TPU v7x, 32 devices: a whole 2x2x4 slice. The times are simulated.
32 devices in a mesh: dp: 4 (over x, core), expert: 8 (over z, y).
Axes of the slice: x: 2, y: 2, z: 4, core: 2. Of those that a mesh axis runs over, the one named last changes fastest.
Arguments:
- tokens: bfloat16 [4096, 768], P(('dp', 'expert')), may hold values from -6 to 6
- segment_ids: int32 [32, 128], P(('dp', 'expert')), may hold values from 0 to 1, never falling along the last dimension, each value on 1 to 96 neighbouring positions
- routes: int32 [4096, 1], P(('dp', 'expert')), may hold values from 0 to 7; in each aligned block of 128 rows (0 to 127, 128 to 255, ...) at most 20 rows name the same one
- bucket_table: int32 [255], replicated, may hold values from 0 to 31
- gain_attn: bfloat16 [768], P(('dp', 'expert')), may hold values from 0.5 to 1.5
- w_query: bfloat16 [768, 768], P(('dp', 'expert')), may hold values from -0.0546875 to 0.0546875
- w_key: bfloat16 [768, 768], P(('dp', 'expert')), may hold values from -0.21875 to 0.21875
- w_value: bfloat16 [768, 768], P(('dp', 'expert')), may hold values from -0.21875 to 0.21875
- w_output: bfloat16 [768, 768], P(('dp', 'expert')), may hold values from -0.875 to 0.875
- rel_bias: float32 [32, 12], replicated, may hold values from -3 to 3
- gain_ffn: bfloat16 [768], P(('dp', 'expert')), may hold values from 0.5 to 1.5
- w_router: bfloat16 [768, 8], P(('dp', 'expert')), may hold values from -0.109375 to 0.109375
- w_in: bfloat16 [8, 768, 3072], P('expert'), may hold values from -0.21875 to 0.21875
- w_out: bfloat16 [8, 3072, 768], P('expert'), may hold values from -4 to 4
- cotangent: bfloat16 [4096, 768], P(('dp', 'expert')), may hold values from -6 to 6
Outputs:
- output: bfloat16 [4096, 768], P(('dp', 'expert'))
- grad_tokens: bfloat16 [4096, 768], P(('dp', 'expert'))
- grad_gain_attn: float32 [768], P(('dp', 'expert'))
- grad_w_query: float32 [768, 768], P(('dp', 'expert'))
- grad_w_key: float32 [768, 768], P(('dp', 'expert'))
- grad_w_value: float32 [768, 768], P(('dp', 'expert'))
- grad_w_output: float32 [768, 768], P(('dp', 'expert'))
- grad_rel_bias: float32 [32, 12], replicated
- grad_gain_ffn: float32 [768], P(('dp', 'expert'))
- grad_w_router: float32 [768, 8], P(('dp', 'expert'))
- grad_w_in: float32 [8, 768, 3072], P('expert', None, 'dp')
- grad_w_out: float32 [8, 3072, 768], P('expert', 'dp')
Inputs may be any that keep to these rules, and one draw needn't show every extreme that they name: `routes`: in the rows of one device no expert is named more than 20 times. `segment_ids`: along a sequence the numbers never fall; a document holds 1 to 96 tokens.
All inputs are finite; a program needn't handle non-finite values.
Results may differ from a plain program's by a relative error of at most 0.018.
Values may be sent and summed in bfloat16 or wider, within the bound.
A program may use at most 128 MiB of HBM per device.

v0:
```python
import jax
import jax.numpy as jnp
from jax import lax
from jax.sharding import PartitionSpec as P

epsilon = 1e-06
highest = lax.Precision.HIGHEST


def gelu_tanh(values):
    return jax.nn.gelu(values, approximate=True)


def bias_table(rel_bias, bucket_table):
    offsets = bucket_table.shape[0]
    length = (offsets + 1) // 2
    onehot = (
        bucket_table[:, None] == jnp.arange(rel_bias.shape[0], dtype=jnp.int32)[None, :]
    ).astype(jnp.float32)
    per_offset = jnp.dot(onehot, rel_bias, precision=highest).T
    padded = jnp.concatenate([per_offset, jnp.zeros((per_offset.shape[0], 1), jnp.float32)], axis=1)
    repeated = jnp.tile(padded, (1, length))[:, : length * offsets]
    return repeated.reshape(per_offset.shape[0], length, offsets)[:, :, length - 1 : offsets]


def norm_back(grad_normed, unit, scale, gain):
    grad_unit = grad_normed * gain
    grad_gain = jnp.sum(grad_normed * unit, axis=0)
    grad_input = scale * (grad_unit - unit * jnp.mean(grad_unit * unit, axis=-1, keepdims=True))
    return (grad_gain, grad_input)


def per_device(
    tokens,
    segment_ids,
    routes,
    bucket_table,
    gain_attn,
    w_query,
    w_key,
    w_value,
    w_output,
    rel_bias,
    gain_ffn,
    w_router,
    w_in,
    w_out,
    cotangent,
):
    length, features = tokens.shape
    num_heads = rel_bias.shape[1]
    head_size = features // num_heads
    local_experts = w_in.shape[0]
    owners = lax.axis_size("expert")
    experts = local_experts * owners
    capacity = 5 * length // (4 * experts)
    gain_one, query_w, key_w, value_w, output_w, router_w, gain_two = (
        lax.all_gather(gain_attn, ("dp", "expert"), axis=0, tiled=True),
        lax.all_gather(w_query, ("dp", "expert"), axis=0, tiled=True),
        lax.all_gather(w_key, ("dp", "expert"), axis=0, tiled=True),
        lax.all_gather(w_value, ("dp", "expert"), axis=0, tiled=True),
        lax.all_gather(w_output, ("dp", "expert"), axis=0, tiled=True),
        lax.all_gather(w_router, ("dp", "expert"), axis=0, tiled=True),
        lax.all_gather(gain_ffn, ("dp", "expert"), axis=0, tiled=True),
    )
    inputs = tokens.astype(jnp.float32)
    scale_one = lax.rsqrt(jnp.mean(inputs * inputs, axis=-1, keepdims=True) + epsilon)
    unit_one = inputs * scale_one
    normed = (unit_one * gain_one.astype(jnp.float32)).astype(jnp.bfloat16)
    query = (
        jnp.dot(normed, query_w, preferred_element_type=jnp.float32)
        .astype(jnp.bfloat16)
        .reshape(length, num_heads, head_size)
    )
    keyed = (
        jnp.dot(normed, key_w, preferred_element_type=jnp.float32)
        .astype(jnp.bfloat16)
        .reshape(length, num_heads, head_size)
    )
    valued = (
        jnp.dot(normed, value_w, preferred_element_type=jnp.float32)
        .astype(jnp.bfloat16)
        .reshape(length, num_heads, head_size)
    )
    pos_bias = bias_table(rel_bias, bucket_table)
    segment = segment_ids[0]
    same_doc = segment[:, None] == segment[None, :]

    def scores_of():
        raw_scores = jnp.einsum("qhe,khe->hqk", query, keyed, preferred_element_type=jnp.float32)
        return jnp.where(same_doc[None], raw_scores + pos_bias, -1e30)

    scores = scores_of()
    row_peak = jnp.max(scores, axis=-1, keepdims=True)
    exp_scores = jnp.exp(scores - row_peak)
    row_total = jnp.sum(exp_scores, axis=-1, keepdims=True)
    attn_probs = exp_scores / row_total
    log_total = row_peak + jnp.log(row_total)
    attended = jnp.einsum(
        "hqk,khe->qhe", attn_probs.astype(jnp.bfloat16), valued, preferred_element_type=jnp.float32
    )
    attended = attended.astype(jnp.bfloat16).reshape(length, features)
    residual = inputs + jnp.dot(attended, output_w, preferred_element_type=jnp.float32)
    scale_two = lax.rsqrt(jnp.mean(residual * residual, axis=-1, keepdims=True) + epsilon)
    unit_two = residual * scale_two
    normed_two = (unit_two * gain_two.astype(jnp.float32)).astype(jnp.bfloat16)
    logits = jnp.dot(normed_two, router_w, preferred_element_type=jnp.float32)
    router_probs = jax.nn.softmax(logits, axis=-1)
    choose = (routes == jnp.arange(experts, dtype=jnp.int32)[None, :]).astype(jnp.float32)
    gate_prob = jnp.sum(router_probs * choose, axis=-1)
    earlier = jnp.cumsum(choose, axis=0) - choose
    position = jnp.sum(earlier * choose, axis=-1).astype(jnp.int32) + routes[:, 0] * capacity
    dispatch = (
        position[:, None] == jnp.arange(experts * capacity, dtype=jnp.int32)[None, :]
    ).astype(jnp.bfloat16)
    slot_shape = (owners, local_experts, capacity, features)
    outgoing = (
        jnp.einsum("lc,ld->cd", dispatch, normed_two, preferred_element_type=jnp.float32)
        .astype(jnp.bfloat16)
        .reshape(slot_shape)
    )
    arrived = lax.all_to_all(outgoing, "expert", split_axis=0, concat_axis=0, tiled=True)
    pre_act = jnp.einsum("secd,edf->secf", arrived, w_in, preferred_element_type=jnp.float32)
    hidden_act = gelu_tanh(pre_act).astype(jnp.bfloat16)
    produced = jnp.einsum(
        "secf,efd->secd", hidden_act, w_out, preferred_element_type=jnp.float32
    ).astype(jnp.bfloat16)
    returned = lax.all_to_all(produced, "expert", split_axis=0, concat_axis=0, tiled=True)
    combined = jnp.einsum(
        "lc,cd->ld",
        dispatch,
        returned.reshape(experts * capacity, features),
        preferred_element_type=jnp.float32,
    )
    output = residual + gate_prob[:, None] * combined
    gain_one, query_w, key_w, value_w, output_w, router_w, gain_two = (
        lax.all_gather(gain_attn, ("dp", "expert"), axis=0, tiled=True),
        lax.all_gather(w_query, ("dp", "expert"), axis=0, tiled=True),
        lax.all_gather(w_key, ("dp", "expert"), axis=0, tiled=True),
        lax.all_gather(w_value, ("dp", "expert"), axis=0, tiled=True),
        lax.all_gather(w_output, ("dp", "expert"), axis=0, tiled=True),
        lax.all_gather(w_router, ("dp", "expert"), axis=0, tiled=True),
        lax.all_gather(gain_ffn, ("dp", "expert"), axis=0, tiled=True),
    )
    upstream = cotangent.astype(jnp.float32)
    grad_combined = (gate_prob[:, None] * upstream).astype(jnp.bfloat16)
    grad_gate = jnp.sum(upstream * combined, axis=-1)
    grad_logits = (grad_gate * gate_prob)[:, None] * (choose - router_probs)
    grad_router = jnp.dot(normed_two.astype(jnp.float32).T, grad_logits, precision=highest)
    grad_normed_router = jnp.dot(grad_logits, router_w.astype(jnp.float32).T, precision=highest)
    grad_slots = (
        jnp.einsum("lc,ld->cd", dispatch, grad_combined, preferred_element_type=jnp.float32)
        .astype(jnp.bfloat16)
        .reshape(slot_shape)
    )
    grad_arrived = lax.all_to_all(grad_slots, "expert", split_axis=0, concat_axis=0, tiled=True)
    grad_hidden = jnp.einsum(
        "secd,efd->secf", grad_arrived, w_out, preferred_element_type=jnp.float32
    )
    gelu_value, gelu_pull = jax.vjp(gelu_tanh, pre_act)
    grad_pre = gelu_pull(grad_hidden)[0].astype(jnp.bfloat16)
    grad_rows = jnp.einsum(
        "secf,edf->secd", grad_pre, w_in, preferred_element_type=jnp.float32
    ).astype(jnp.bfloat16)
    grad_returned = lax.all_to_all(grad_rows, "expert", split_axis=0, concat_axis=0, tiled=True)
    grad_normed_expert = jnp.einsum(
        "lc,cd->ld",
        dispatch,
        grad_returned.reshape(experts * capacity, features),
        preferred_element_type=jnp.float32,
    )
    rows_all, grads_all = (
        lax.all_gather(arrived, "dp", axis=0, tiled=True),
        lax.all_gather(grad_arrived, "dp", axis=0, tiled=True),
    )
    pre_part, act_part = (
        lax.all_to_all(grad_pre, "dp", split_axis=3, concat_axis=0, tiled=True),
        lax.all_to_all(hidden_act, "dp", split_axis=3, concat_axis=0, tiled=True),
    )
    grad_first_w = jnp.einsum(
        "secd,secf->edf", rows_all, pre_part, preferred_element_type=jnp.float32
    )
    grad_second_w = jnp.einsum(
        "secf,secd->efd", act_part, grads_all, preferred_element_type=jnp.float32
    )
    grad_normed_two = grad_normed_router + grad_normed_expert
    grad_gain_two, grad_through = norm_back(
        grad_normed_two, unit_two, scale_two, gain_two.astype(jnp.float32)
    )
    grad_residual = upstream + grad_through
    grad_attn = grad_residual.astype(jnp.bfloat16)
    grad_output_w = jnp.einsum("ld,le->de", attended, grad_attn, preferred_element_type=jnp.float32)
    grad_attended = (
        jnp.einsum("le,de->ld", grad_attn, output_w, preferred_element_type=jnp.float32)
        .astype(jnp.bfloat16)
        .reshape(length, num_heads, head_size)
    )
    attn_probs = jnp.exp(scores_of() - log_total)
    grad_value = jnp.einsum(
        "hqk,qhe->khe",
        attn_probs.astype(jnp.bfloat16),
        grad_attended,
        preferred_element_type=jnp.float32,
    ).astype(jnp.bfloat16)
    grad_probs = jnp.einsum(
        "qhe,khe->hqk", grad_attended, valued, preferred_element_type=jnp.float32
    )
    grad_scores = attn_probs * (
        grad_probs - jnp.sum(grad_probs * attn_probs, axis=-1, keepdims=True)
    )
    bias_value, bias_pull = jax.vjp(
        lambda table_bias: bias_table(table_bias, bucket_table), rel_bias
    )
    grad_rel = bias_pull(grad_scores)[0]
    scores_low = grad_scores.astype(jnp.bfloat16)
    grad_query = (
        jnp.einsum("hqk,khe->qhe", scores_low, keyed, preferred_element_type=jnp.float32)
        .astype(jnp.bfloat16)
        .reshape(length, features)
    )
    grad_key = (
        jnp.einsum("hqk,qhe->khe", scores_low, query, preferred_element_type=jnp.float32)
        .astype(jnp.bfloat16)
        .reshape(length, features)
    )
    grad_value = grad_value.reshape(length, features)
    grad_query_w = jnp.einsum("ld,le->de", normed, grad_query, preferred_element_type=jnp.float32)
    grad_key_w = jnp.einsum("ld,le->de", normed, grad_key, preferred_element_type=jnp.float32)
    grad_value_w = jnp.einsum("ld,le->de", normed, grad_value, preferred_element_type=jnp.float32)
    grad_normed_one = jnp.einsum(
        "le,de->ld", grad_query, query_w, preferred_element_type=jnp.float32
    )
    grad_normed_one = grad_normed_one + jnp.einsum(
        "le,de->ld", grad_key, key_w, preferred_element_type=jnp.float32
    )
    grad_normed_one = grad_normed_one + jnp.einsum(
        "le,de->ld", grad_value, value_w, preferred_element_type=jnp.float32
    )
    grad_gain_one, grad_inner = norm_back(
        grad_normed_one, unit_one, scale_one, gain_one.astype(jnp.float32)
    )
    grad_inputs = grad_residual + grad_inner
    reduced = (
        lax.psum_scatter(grad_gain_one, ("dp", "expert"), scatter_dimension=0, tiled=True),
        lax.psum_scatter(grad_query_w, ("dp", "expert"), scatter_dimension=0, tiled=True),
        lax.psum_scatter(grad_key_w, ("dp", "expert"), scatter_dimension=0, tiled=True),
        lax.psum_scatter(grad_value_w, ("dp", "expert"), scatter_dimension=0, tiled=True),
        lax.psum_scatter(grad_output_w, ("dp", "expert"), scatter_dimension=0, tiled=True),
        lax.psum_scatter(grad_router, ("dp", "expert"), scatter_dimension=0, tiled=True),
        lax.psum_scatter(grad_gain_two, ("dp", "expert"), scatter_dimension=0, tiled=True),
    )
    grad_rel_all = lax.psum(grad_rel, ("dp", "expert"))
    return (
        output.astype(jnp.bfloat16),
        grad_inputs.astype(jnp.bfloat16),
        reduced[0],
        reduced[1],
        reduced[2],
        reduced[3],
        reduced[4],
        grad_rel_all,
        reduced[6],
        reduced[5],
        grad_first_w,
        grad_second_w,
    )


def solution(mesh):
    return jax.shard_map(
        per_device,
        mesh=mesh,
        in_specs=(
            P(("dp", "expert"), None),
            P(("dp", "expert"), None),
            P(("dp", "expert"), None),
            P(),
            P(("dp", "expert")),
            P(("dp", "expert"), None),
            P(("dp", "expert"), None),
            P(("dp", "expert"), None),
            P(("dp", "expert"), None),
            P(),
            P(("dp", "expert")),
            P(("dp", "expert"), None),
            P("expert", None, None),
            P("expert", None, None),
            P(("dp", "expert"), None),
        ),
        out_specs=(
            P(("dp", "expert"), None),
            P(("dp", "expert"), None),
            P(("dp", "expert")),
            P(("dp", "expert"), None),
            P(("dp", "expert"), None),
            P(("dp", "expert"), None),
            P(("dp", "expert"), None),
            P(),
            P(("dp", "expert")),
            P(("dp", "expert"), None),
            P("expert", None, "dp"),
            P("expert", "dp", None),
        ),
        check_vma=False,
    )
```

profile of v0, /device:TPU:0, one launch (start us, length us, event | category | flops | bytes accessed | tf_op | source)
XLA Modules:
  0.0 728.0 jit_solution(50092980029665326)
XLA Ops:
  7.2 0.7 all-gather.6.cloned.1.call-update
  8.0 0.7 all-gather.8.cloned.1.call-update
  8.7 0.7 all-gather.10.cloned.1.call-update
  10.0 0.9 convolution_bitcast_fusion.2
  10.9 0.8 dynamic-update-slice
  11.8 0.8 dynamic-update-slice.1
  12.6 42.1 %all-reduce.9 = (bf16[768]{0:T(1024)(128)(2,1)S(1)}, bf16[768]{0:T(1024)(128)(2,1)S(1)}) all-reduce(bf16[768]{0:T(1024)(128)(2,1)S(1)} %dynamic-update-slice, bf16[768]{0:T(1024)(128)(2,1)S(1)} %dynamic-update-slice.1), channel_id=1, replica_groups=mesh['dp'=4,'expert'=8] {'dp','expert'}, use_global_device_ids=true, to_apply=%add.3 | all-reduce | flops 1536 | bytes 6144
  55.1 1.2 copy.100
  56.4 3.3 reshape.203
  59.8 1.7 slice.9
  61.8 66.2 %all-gather = bf16[32,24,8]{1,2,0:T(8,128)(2,1)S(1)} all-gather(bf16[1,24,8]{1,2,0:T(8,128)(2,1)S(1)} %bitcast.203), channel_id=1, replica_groups=mesh['dp'=4,'expert'=8] {'dp','expert'}, dimensions={0}, use_global_device_ids=true | all-gather | bytes 12672 | tf_op jit(solution)/shard_map/all_gather | solution.py:63
  128.8 1.7 convolution_convert_fusion.9
  130.7 1.7 convolution_convert_fusion.8
  132.6 47.3 %all-gather.10.cloned.1.call-done = bf16[768,768]{1,0:T(8,128)(2,1)} async-done(((bf16[24,768]{1,0:T(8,128)(2,1)}), bf16[768,768]{1,0:T(8,128)(2,1)}) %all-gather.10.cloned.1.call-update) | async-done | bytes 1179664 | tf_op jit(solution)/shard_map/all_gather | solution.py:60
  179.9 1.7 convolution_convert_fusion.7
  182.5 53.2 %all-gather.12.cloned.1.call-done = bf16[768,768]{1,0:T(8,128)(2,1)} async-done(((bf16[24,768]{1,0:T(8,128)(2,1)}), bf16[768,768]{1,0:T(8,128)(2,1)}) %all-gather.12.cloned.1.call-update) | async-done | bytes 1179664 | tf_op jit(solution)/shard_map/all_gather | solution.py:62
  235.8 1.7 multiply_reduce_fusion.3
  239.2 0.8 reshape.205
  239.9 4.4 all-to-all-start
  244.7 0.8 reshape.211
  245.5 8.9 %all-to-all-done = bf16[8,1,20,768]{3,2,1,0:T(8,128)(2,1)S(1)} async-done(((bf16[8,1,20,768]{3,2,1,0:T(8,128)(2,1)}), bf16[8,1,20,768]{3,2,1,0:T(8,128)(2,1)S(1)}, u32[]{:S(2)}, u32[]{:S(2)}) %all-to-all-start) | async-done | bytes 245792 | tf_op jit(solution)/shard_map/all_to_all | solution.py:122
  254.3 3.6 all-to-all-start.2
  258.0 5.2 multiply_convert_fusion
  263.2 4.7 fusion.34
  267.9 6.2 all-to-all-start.1
  274.1 5.4 fusion.20
  279.6 5.2 fusion.39
  284.8 6.2 all-to-all-start.3
  291.1 1.7 fusion.61
  292.8 0.8 mul.209
  293.5 1.1 fusion.87
  294.6 5.1 all-to-all-done.3
  299.8 1.7 reshape.214
  301.5 1.3 multiply_reduce_fusion.1
  302.8 1.9 convert_add_fusion
  305.4 1.3 multiply_reduce_fusion
  307.2 2.0 fusion.99
  309.6 1.9 fusion.97
  312.5 2.0 fusion.95
  314.5 7.0 copy.83
  321.6 5.8 copy.86
  327.4 15.2 %reshape.237 = bf16[4,2,61440]{2,1,0:T(2,128)(2,1)} reshape(bf16[3072,1,8,20]{3,2,1,0:T(8,128)(2,1)} %bitcast.173) | data formatting | bytes 1966080
  342.6 4.2 all-to-all-start.4
  346.9 15.2 %reshape.239 = bf16[4,2,61440]{2,1,0:T(2,128)(2,1)} reshape(bf16[3072,1,8,20]{3,2,1,0:T(8,128)(2,1)} %bitcast.172) | data formatting | bytes 1966080
  362.3 10.5 %all_gather.41 = bf16[32,1,20,768]{3,0,2,1:T(8,128)(2,1)} all-gather(bf16[8,1,20,768]{3,0,2,1:T(8,128)(2,1)S(1)} %copy.81), channel_id=1, replica_groups=mesh['dp'=4,'expert'=8] {'dp'}, dimensions={0}, use_global_device_ids=true | all-gather | bytes 1228800 | tf_op jit(solution)/shard_map/all_gather | solution.py:173
  372.8 11.4 %all_gather.42 = bf16[32,1,20,768]{3,0,2,1:T(8,128)(2,1)} all-gather(bf16[8,1,20,768]{3,0,2,1:T(8,128)(2,1)S(1)} %copy.89), channel_id=1, replica_groups=mesh['dp'=4,'expert'=8] {'dp'}, dimensions={0}, use_global_device_ids=true | all-gather | bytes 1228800 | tf_op jit(solution)/shard_map/all_gather | solution.py:174
  384.3 1.9 fusion.73
  386.2 1.3 fusion.106
  388.0 1.6 pad.7.clone
  389.6 2.5 reshape.219
  394.4 0.6 fusion.59
  395.1 3.5 all-to-all-start.5
  398.8 46.4 %all-reduce.8 = (f32[768]{0:T(1024)S(1)}, f32[32,12]{0,1:T(8,128)}, f32[768]{0:T(1024)S(1)}, f32[768,8]{0,1:T(8,128)S(1)}) all-reduce(f32[768]{0:T(1024)S(1)} %get-tuple-element.14, f32[32,12]{0,1:T(8,128)S(1)} %fusion.72, f32[768]{0:T(1024)S(1)} %get-tuple-element.12, ...), channel_id=2, replica_groups=mesh['dp'=4,'expert'=8] {'dp','expert'}, use_global_device_ids=true, to_apply=%region_14.15.clone | all-reduce | flops 8064 | bytes 64512
  446.4 0.7 constant_dynamic-slice_fusion
  447.1 0.9 fusion.58
  448.0 18.1 %reshape.238 = bf16[3072,1,8,20]{3,2,1,0:T(8,128)(2,1)} reshape(bf16[4,2,61440]{2,1,0:T(2,128)(2,1)} %all-to-all-done.4) | data formatting | bytes 1966080
  466.1 7.4 %copy.94 = bf16[8,1,20,4,768]{4,3,0,2,1:T(4,128)(2,1)S(1)} copy(bf16[8,1,20,4,768]{2,0,4,3,1:T(8,128)(2,1)} %bitcast.174) | data formatting | bytes 1966080 | tf_op jit(solution)/shard_map/all_to_all | solution.py:177
  474.1 17.3 %reshape.240 = bf16[3072,1,8,20]{3,2,1,0:T(8,128)(2,1)} reshape(bf16[4,2,61440]{2,1,0:T(2,128)(2,1)S(1)} %all-to-all-done.5) | data formatting | bytes 1966080
  491.4 7.4 %copy.95 = bf16[8,1,20,4,768]{4,3,0,2,1:T(4,128)(2,1)S(1)} copy(bf16[8,1,20,4,768]{2,0,4,3,1:T(8,128)(2,1)} %bitcast.175) | data formatting | bytes 1966080 | tf_op jit(solution)/shard_map/all_to_all | solution.py:178
  498.9 3.8 convolution_bitcast_fusion
  502.7 2.8 convolution_bitcast_fusion.1
  505.5 6.8 reduce-scatter.8.cloned.1.call-done
  512.3 103.9 %reduce-scatter.10.cloned.1.call-done = f32[24,768]{1,0:T(8,128)} async-done(((f32[768,768]{1,0:T(8,128)}), f32[24,768]{1,0:T(8,128)}) %reduce-scatter.10.cloned.1.call-update) | async-done | bytes 73744 | tf_op jit(solution)/shard_map/reduce_scatter | solution.py:247
  616.2 104.7 %reduce-scatter.12.cloned.1.call-done = f32[24,768]{1,0:T(8,128)} async-done(((f32[768,768]{1,0:T(8,128)}), f32[24,768]{1,0:T(8,128)}) %reduce-scatter.12.cloned.1.call-update) | async-done | bytes 73744 | tf_op jit(solution)/shard_map/reduce_scatter | solution.py:248
  (178 shorter events, 12.7 us)
Async XLA Ops:
  7.2 2.8 copy-start
  7.2 121.6 %all-gather.6.cloned.1.call-start = ((), (), s32[]{:S(2)}) async-start(), calls=%async_computation.10 | async-start | bytes 1216512 | tf_op jit(solution)/shard_map/all_gather | solution.py:61
  7.9 122.7 %all-gather.8.cloned.1.call-start = ((), (), s32[]{:S(2)}) async-start(), calls=%async_computation.11 | async-start | bytes 1216512 | tf_op jit(solution)/shard_map/all_gather | solution.py:59
  8.7 171.2 %all-gather.10.cloned.1.call-start = ((), (), s32[]{:S(2)}) async-start(), calls=%async_computation.12 | async-start | bytes 1216512 | tf_op jit(solution)/shard_map/all_gather | solution.py:60
  9.4 226.4 %all-gather.12.cloned.1.call-start = ((), (), s32[]{:S(2)}) async-start(), calls=%async_computation.13 | async-start | bytes 1216512 | tf_op jit(solution)/shard_map/all_gather | solution.py:62
  59.8 2.0 copy-start.49
  59.8 68.4 %copy-start.39 = (s32[128,1]{0,1:T(1,128)S(1)}, s32[128,1]{0,1:T(1,128)}, u32[]{:S(2)}) copy-start(s32[128,1]{0,1:T(1,128)} %param.17) | copy-start | bytes 1540
  59.8 68.7 %copy-start.2 = (bf16[128,768]{1,0:T(8,128)(2,1)S(1)}, bf16[128,768]{1,0:T(8,128)(2,1)}, u32[]{:S(2)}) copy-start(bf16[128,768]{1,0:T(8,128)(2,1)} %param.15) | copy-start | bytes 589828
  59.8 68.9 %copy-start.50 = (s32[1,128]{1,0:T(1,128)S(1)}, s32[1,128]{1,0:T(1,128)}, u32[]{:S(2)}) copy-start(s32[1,128]{1,0:T(1,128)} %param.16) | copy-start | bytes 1540
  61.8 175.7 %copy-start.33 = (f32[768]{0:T(1024)}, f32[768]{0:T(1024)S(1)}, u32[]{:S(2)}) copy-start(f32[768]{0:T(1024)S(1)} %convert_element_type.143) | copy-start | bytes 9220
  128.2 110.0 %copy-start.32 = (bf16[768,8]{0,1:T(8,128)(2,1)}, bf16[768,8]{0,1:T(8,128)(2,1)S(1)}, u32[]{:S(2)}) copy-start(bf16[768,8]{0,1:T(8,128)(2,1)S(1)} %reshape.230) | copy-start | bytes 36868
  128.7 51.2 %copy-start.35 = (f32[128]{0:T(128)}, f32[128]{0:T(128)S(1)}, u32[]{:S(2)}) copy-start(f32[128]{0:T(128)S(1)} %add_rsqrt_fusion.1) | copy-start | bytes 1540
  130.6 51.6 %copy-start.31 = (bf16[128,768]{0,1:T(8,128)(2,1)}, bf16[128,768]{0,1:T(8,128)(2,1)S(1)}, u32[]{:S(2)}) copy-start(bf16[128,768]{0,1:T(8,128)(2,1)S(1)} %copy.64) | copy-start | bytes 589828
  181.7 0.8 copy-start.16
  182.5 55.9 %copy-start.29 = (bf16[12,64,128]{2,1,0:T(8,128)(2,1)}, bf16[12,64,128]{2,1,0:T(8,128)(2,1)S(1)}, u32[]{:S(2)}) copy-start(bf16[12,64,128]{2,1,0:T(8,128)(2,1)S(1)} %convolution_convert_fusion.6) | copy-start | bytes 589828
  182.5 61.8 %copy-start.15 = (bf16[128,768]{1,0:T(8,128)(2,1)S(1)}, bf16[128,768]{1,0:T(8,128)(2,1)}, u32[]{:S(2)}) copy-start(bf16[128,768]{1,0:T(8,128)(2,1)} %param.29) | copy-start | bytes 589828
  238.3 1.6 copy-start.37
  238.4 1.6 copy-start.41
  238.4 15.9 %copy-start.45 = (f32[128]{0:T(128)}, f32[128]{0:T(128)S(1)}, u32[]{:S(2)}) copy-start(f32[128]{0:T(128)S(1)} %get-tuple-element.16) | copy-start | bytes 1540
  238.8 15.5 %copy-start.43 = (s32[128]{0:T(128)}, s32[128]{0:T(128)S(1)}, u32[]{:S(2)}) copy-start(s32[128]{0:T(128)S(1)} %fusion.92) | copy-start | bytes 1540
  239.9 14.4 %all-to-all-start = ((bf16[8,1,20,768]{3,2,1,0:T(8,128)(2,1)}), bf16[8,1,20,768]{3,2,1,0:T(8,128)(2,1)S(1)}, u32[]{:S(2)}, u32[]{:S(2)}) async-start(bf16[8,1,20,768]{3,2,1,0:T(8,128)(2,1)} %bitcast.11), calls=%async_computation | async-start | bytes 589824 | tf_op jit(solution)/shard_map/all_to_all | solution.py:122
  254.3 8.9 %copy-start.24 = (bf16[8,1,20,768]{3,2,1,0:T(8,128)(2,1)}, bf16[8,1,20,768]{3,2,1,0:T(8,128)(2,1)S(1)}, u32[]{:S(2)}) copy-start(bf16[8,1,20,768]{3,2,1,0:T(8,128)(2,1)S(1)} %all-to-all-done) | copy-start | bytes 737284
  254.3 13.5 %all-to-all-start.2 = ((bf16[8,1,20,768]{3,2,1,0:T(8,128)(2,1)}), bf16[8,1,20,768]{3,2,1,0:T(8,128)(2,1)S(1)}, u32[]{:S(2)}, u32[]{:S(2)}) async-start(bf16[8,1,20,768]{3,2,1,0:T(8,128)(2,1)} %bitcast.27), calls=%async_computation.2 | async-start | bytes 589824 | tf_op jit(solution)/shard_map/all_to_all | solution.py:156
  263.2 4.7 copy-start.21
  267.9 11.7 %copy-start.26 = (bf16[8,1,20,768]{3,2,1,0:T(8,128)(2,1)}, bf16[8,1,20,768]{3,2,1,0:T(8,128)(2,1)S(1)}, u32[]{:S(2)}) copy-start(bf16[8,1,20,768]{3,2,1,0:T(8,128)(2,1)S(1)} %all-to-all-done.2) | copy-start | bytes 737284
  267.9 17.0 %all-to-all-start.1 = ((bf16[8,1,20,768]{3,2,1,0:T(8,128)(2,1)}), bf16[8,1,20,768]{3,2,1,0:T(8,128)(2,1)S(1)}, u32[]{:S(2)}, u32[]{:S(2)}) async-start(bf16[8,1,20,768]{3,2,1,0:T(8,128)(2,1)} %fusion.34), calls=%async_computation.1 | async-start | bytes 589824 | tf_op jit(solution)/shard_map/all_to_all | solution.py:128
  279.6 5.2 copy-start.23
  284.8 16.7 %copy-start.34 = (f32[768]{0:T(1024)S(1)}, f32[768]{0:T(1024)}, u32[]{:S(2)}) copy-start(f32[768]{0:T(1024)} %copy-done.33) | copy-start | bytes 9220
  284.8 16.7 %copy-start.44 = (s32[128]{0:T(128)S(1)}, s32[128]{0:T(128)}, u32[]{:S(2)}) copy-start(s32[128]{0:T(128)} %copy-done.43) | copy-start | bytes 1540
  284.8 16.7 %copy-start.48 = (f32[128]{0:T(128)S(1)}, f32[128]{0:T(128)}, u32[]{:S(2)}) copy-start(f32[128]{0:T(128)} %copy-done.47) | copy-start | bytes 1540
  284.8 18.0 %copy-start.46 = (f32[128]{0:T(128)S(1)}, f32[128]{0:T(128)}, u32[]{:S(2)}) copy-start(f32[128]{0:T(128)} %copy-done.45) | copy-start | bytes 1540
  284.8 14.9 %all-to-all-start.3 = ((bf16[8,1,20,768]{3,2,1,0:T(8,128)(2,1)}), bf16[8,1,20,768]{3,2,1,0:T(8,128)(2,1)}, u32[]{:S(2)}, u32[]{:S(2)}) async-start(bf16[8,1,20,768]{3,2,1,0:T(8,128)(2,1)} %fusion.39), calls=%async_computation.3 | async-start | bytes 589824 | tf_op jit(solution)/shard_map/all_to_all | solution.py:165
  291.0 214.5 %reduce-scatter.6.cloned.1.call-start = ((), (), s32[]{:S(2)}) async-start(), calls=%async_computation.14 | async-start | bytes 2433024 | tf_op jit(solution)/shard_map/reduce_scatter | solution.py:245
  292.8 11.9 %copy-start.6 = (bf16[768,768]{1,0:T(8,128)(2,1)S(1)}, bf16[768,768]{1,0:T(8,128)(2,1)}, u32[]{:S(2)}) copy-start(bf16[768,768]{1,0:T(8,128)(2,1)} %all-gather.12.cloned.1.call-done) | copy-start | bytes 3538948
  305.2 1.7 copy-start.17
  305.4 1.4 copy-start.18
  305.4 1.8 copy-start.36
  307.2 2.0 copy-start.13
  309.2 203.1 %reduce-scatter.8.cloned.1.call-start = ((), (), s32[]{:S(2)}) async-start(), calls=%async_computation.15 | async-start | bytes 2433024 | tf_op jit(solution)/shard_map/reduce_scatter | solution.py:246
  309.6 2.0 copy-start.9
  309.6 2.5 copy-start.19
  311.6 304.6 %reduce-scatter.10.cloned.1.call-start = ((), (), s32[]{:S(2)}) async-start(), calls=%async_computation.16 | async-start | bytes 2433024 | tf_op jit(solution)/shard_map/reduce_scatter | solution.py:247
  312.5 2.0 copy-start.11
  314.5 7.0 copy-start.22
  342.6 52.5 %all-to-all-start.4 = ((bf16[4,2,61440]{2,1,0:T(2,128)(2,1)}), bf16[4,2,61440]{2,1,0:T(2,128)(2,1)}, u32[]{:S(2)}, u32[]{:S(2)}) async-start(bf16[4,2,61440]{2,1,0:T(2,128)(2,1)} %reshape.237), calls=%async_computation.8 | async-start | bytes 1966080 | tf_op jit(solution)/shard_map/all_to_all | solution.py:177
  346.8 374.1 %reduce-scatter.12.cloned.1.call-start = ((), (), s32[]{:S(2)}) async-start(), calls=%async_computation.17 | async-start | bytes 2433024 | tf_op jit(solution)/shard_map/reduce_scatter | solution.py:248
  346.9 15.3 %copy-start.25 = (bf16[8,1,20,768]{3,2,1,0:T(8,128)(2,1)S(1)}, bf16[8,1,20,768]{3,2,1,0:T(8,128)(2,1)}, u32[]{:S(2)}) copy-start(bf16[8,1,20,768]{3,2,1,0:T(8,128)(2,1)} %copy-done.24) | copy-start | bytes 737284
  346.9 15.3 %copy-start.27 = (bf16[8,1,20,768]{3,2,1,0:T(8,128)(2,1)S(1)}, bf16[8,1,20,768]{3,2,1,0:T(8,128)(2,1)}, u32[]{:S(2)}) copy-start(bf16[8,1,20,768]{3,2,1,0:T(8,128)(2,1)} %copy-done.26) | copy-start | bytes 737284
  362.2 22.1 %copy-start.30 = (bf16[12,64,128]{2,1,0:T(8,128)(2,1)S(1)}, bf16[12,64,128]{2,1,0:T(8,128)(2,1)}, u32[]{:S(2)}) copy-start(bf16[12,64,128]{2,1,0:T(8,128)(2,1)} %copy-done.29) | copy-start | bytes 589828
  384.3 2.0 copy-start.5
  384.3 2.0 copy-start.14
  386.2 1.3 copy-start.8
  386.2 1.3 copy-start.38
  386.2 1.3 copy-start.40
  386.2 1.3 copy-start.42
  392.3 1.3 copy-start.4
  392.3 1.3 copy-start.10
  392.3 1.4 copy-start.20
  393.0 1.4 copy-start.3
  393.0 1.4 copy-start.12
  394.4 4.2 copy-start.51
  395.1 79.0 %all-to-all-start.5 = ((bf16[4,2,61440]{2,1,0:T(2,128)(2,1)}), bf16[4,2,61440]{2,1,0:T(2,128)(2,1)S(1)}, u32[]{:S(2)}, u32[]{:S(2)}) async-start(bf16[4,2,61440]{2,1,0:T(2,128)(2,1)} %reshape.239), calls=%async_computation.9 | async-start | bytes 1966080 | tf_op jit(solution)/shard_map/all_to_all | solution.py:178
  498.8 3.8 copy-start.28
  502.7 218.3 %copy-start.1 = (f32[32,12]{0,1:T(8,128)S(1)}, f32[32,12]{0,1:T(8,128)}, u32[]{:S(2)}) copy-start(f32[32,12]{0,1:T(8,128)} %param.24) | copy-start | bytes 4612
  (2 other events, 1.2 us)
Sparse Core Ops, SparseCore 0:
  10.9 56.8 all-gather.5
  70.8 52.9 all-gather.7
  126.7 53.1 all-gather.9
  182.7 53.0 all-gather.11
  309.3 98.3 reduce-scatter.5
  414.2 97.9 reduce-scatter.7
  518.1 98.0 reduce-scatter.9
  622.9 97.9 reduce-scatter.11
where the time goes:
time: 738 us; the launch traced here: 728 us
  waiting for transfers between devices  333 us (45%)
  blocking collectives  177 us (24%)
  local copies, waits for them, and re-layouts  116 us (16%)
  matrix products  53.8 us (7%)
  starting transfers between devices  28.9 us (4%)
  between operations  15.2 us (2%)
    reduce_scatter x1, waiting for transfers between devices, per_device(): lax.psum_scatter(grad_output_w, ('dp', 'expert'), scatter_dimension=0, ti...  105 us
    reduce_scatter x1, waiting for transfers between devices, per_device(): lax.psum_scatter(grad_value_w, ('dp', 'expert'), scatter_dimension=0, til...  104 us
    unnamed x2, blocking collectives  88.5 us
    unnamed x121, local copies, waits for them, and re-layouts  74 us
    all_gather x1, blocking collectives, per_device(): lax.all_gather(w_router, ('dp', 'expert'), axis=0, tiled=True)  66.2 us
    all_gather x1, waiting for transfers between devices, per_device(): lax.all_gather(w_output, ('dp', 'expert'), axis=0, tiled=True)  53.2 us
    all_gather x1, waiting for transfers between devices, per_device(): lax.all_gather(w_key, ('dp', 'expert'), axis=0, tiled=True)  47.3 us
  transfers between devices with their start and end apart: 14, of which 7 were waited for; matrix products, arithmetic and copies ran while one was open for 22% of the time, Pallas kernels for 0%

commit v1 on v0

--- a/solution.py
+++ b/solution.py
@@ -1,6 +1,10 @@
+import functools
+
 import jax
 import jax.numpy as jnp
 from jax import lax
+from jax.experimental import pallas as pl
+from jax.experimental.pallas import tpu as pltpu
 from jax.sharding import PartitionSpec as P
 
 epsilon = 1e-06
@@ -28,6 +32,243 @@
     grad_gain = jnp.sum(grad_normed * unit, axis=0)
     grad_input = scale * (grad_unit - unit * jnp.mean(grad_unit * unit, axis=-1, keepdims=True))
     return (grad_gain, grad_input)
+
+
+def doubling(count):
+    return [2**step for step in range(count.bit_length() - 1)]
+
+
+def exchange_orders(dp_size, expert_size):
+    x_size = dp_size // 2
+    y_size = min(x_size, expert_size)
+    z_size = expert_size // y_size
+    along_y = doubling(y_size)
+    along_z = [y_size * step for step in doubling(z_size)]
+    cores = [expert_size]
+    along_x = [2 * expert_size * step for step in doubling(x_size)]
+    return (along_z + along_y + along_x + cores, along_z + along_x + along_y + cores)
+
+
+def signed(me, weight):
+    return weight * (1 - 2 * ((me // weight) % 2))
+
+
+def member(me, order, slot):
+    other = me
+    for step, weight in enumerate(order):
+        other = other + ((slot // 2**step) % 2) * signed(me, weight)
+    return other
+
+
+def device_of(index, expert_size):
+    return (index // expert_size, index % expert_size)
+
+
+def meet(me, weights, expert_size):
+    barrier = pltpu.get_barrier_semaphore()
+    for weight in weights:
+        pl.semaphore_signal(
+            barrier,
+            inc=1,
+            device_id=device_of(me + signed(me, weight), expert_size),
+            device_id_type=pl.DeviceIdType.MESH,
+        )
+    pl.semaphore_wait(barrier, len(weights))
+
+
+def send(me, weight, expert_size, source, target, send_sem, recv_sem):
+    copy = pltpu.make_async_remote_copy(
+        src_ref=source,
+        dst_ref=target,
+        send_sem=send_sem,
+        recv_sem=recv_sem,
+        device_id=device_of(me + signed(me, weight), expert_size),
+        device_id_type=pl.DeviceIdType.MESH,
+    )
+    copy.start()
+    return copy
+
+
+def gather_kernel(orders, expert_size, *refs):
+    shards, outs, held, sems = refs[:2], refs[2:4], refs[4:6], refs[6:]
+    send_sem, recv_sem = sems
+    me = lax.axis_index("dp") * expert_size + lax.axis_index("expert")
+    stages = len(orders[0])
+    for shard, buffer in zip(shards, held):
+        buffer[0] = shard[...]
+    meet(me, orders[0], expert_size)
+    copies = [[], []]
+    for stage in range(stages):
+        size = 2**stage
+        for part in range(2):
+            if stage:
+                copies[part][-1].wait_recv()
+            copies[part].append(
+                send(
+                    me,
+                    orders[part][stage],
+                    expert_size,
+                    held[part].at[pl.ds(0, size)],
+                    held[part].at[pl.ds(size, size)],
+                    send_sem.at[part, stage],
+                    recv_sem.at[part, stage],
+                )
+            )
+
+    def place(part, first, last):
+        def body(slot, carry):
+            outs[part][member(me, orders[part], slot)] = held[part][slot]
+            return carry
+
+        lax.fori_loop(first, last, body, 0)
+
+    half = 2 ** (stages - 1)
+    for part in range(2):
+        place(part, 0, half)
+    for part in range(2):
+        copies[part][-1].wait_recv()
+        place(part, half, 2 * half)
+    for part in range(2):
+        for copy in copies[part]:
+            copy.wait_send()
+
+
+def gather_shards(shards, dp_size, expert_size):
+    count = dp_size * expert_size
+    orders = exchange_orders(dp_size, expert_size)
+    stages = len(orders[0])
+    shapes = [(count,) + shard.shape for shard in shards]
+    vmem = pl.BlockSpec(memory_space=pltpu.VMEM)
+    return pl.pallas_call(
+        functools.partial(gather_kernel, orders, expert_size),
+        out_shape=[jax.ShapeDtypeStruct(shape, jnp.bfloat16) for shape in shapes],
+        in_specs=[vmem] * 2,
+        out_specs=[vmem] * 2,
+        scratch_shapes=[pltpu.VMEM(shape, jnp.bfloat16) for shape in shapes]
+        + [pltpu.SemaphoreType.DMA((2, stages)), pltpu.SemaphoreType.DMA((2, stages))],
+        compiler_params=pltpu.CompilerParams(
+            collective_id=0, has_side_effects=True, vmem_limit_bytes=40 * 2**20
+        ),
+    )(*shards)
+
+
+def scatter_kernel(orders, expert_size, *refs):
+    grads, small, outs, small_out = refs[:2], refs[2], refs[3:5], refs[5]
+    held, landed, small_held, small_landed = refs[6:8], refs[8:10], refs[10], refs[11]
+    send_sem, recv_sem = refs[12:]
+    me = lax.axis_index("dp") * expert_size + lax.axis_index("expert")
+    stages = len(orders[0])
+    count = 2**stages
+    half = count // 2
+
+    def fill(part, first, last):
+        def body(slot, carry):
+            held[part][slot] = grads[part][member(me, orders[part], slot)]
+            return carry
+
+        lax.fori_loop(first, last, body, 0)
+
+    def start(part, stage):
+        size = 2**stage
+        return send(
+            me,
+            orders[part][stage],
+            expert_size,
+            held[part].at[pl.ds(size, size)],
+            landed[part].at[pl.ds(size, size)],
+            send_sem.at[part, stage],
+            recv_sem.at[part, stage],
+        )
+
+    def start_small(stage):
+        return send(
+            me,
+            orders[0][stage],
+            expert_size,
+            small_held.at[stage],
+            small_landed.at[stage],
+            send_sem.at[2, stage],
+            recv_sem.at[2, stage],
+        )
+
+    small_held[stages - 1] = small[...]
+    fill(0, half, count)
+    meet(me, orders[0], expert_size)
+    started = [start(0, stages - 1)]
+    fill(1, half, count)
+    started.append(start(1, stages - 1))
+    small_copy = start_small(stages - 1)
+    fill(0, 0, half)
+    fill(1, 0, half)
+    sent = []
+    current = list(started)
+    for stage in reversed(range(stages)):
+        size = 2**stage
+        for part in range(2):
+            current[part].wait_recv()
+            sent.append(current[part])
+            if stage:
+
+                def body(slot, carry):
+                    held[part][slot] = (
+                        held[part][slot].astype(jnp.float32)
+                        + landed[part][slot + size].astype(jnp.float32)
+                    ).astype(jnp.bfloat16)
+                    return carry
+
+                lax.fori_loop(size // 2, size, body, 0)
+                current[part] = start(part, stage - 1)
+                lax.fori_loop(0, size // 2, body, 0)
+            else:
+                outs[part][...] = held[part][0].astype(jnp.float32) + landed[part][1].astype(
+                    jnp.float32
+                )
+        small_copy.wait_recv()
+        sent.append(small_copy)
+        total = small_held[stage] + small_landed[stage]
+        if stage:
+            small_held[stage - 1] = total
+            small_copy = start_small(stage - 1)
+        else:
+            small_out[...] = total
+    for copy in sent:
+        copy.wait_send()
+
+
+def scatter_sums(grads, small, dp_size, expert_size):
+    orders = exchange_orders(dp_size, expert_size)
+    stages = len(orders[0])
+    shapes = [grad.shape for grad in grads]
+    vmem = pl.BlockSpec(memory_space=pltpu.VMEM)
+    buffers = [pltpu.VMEM(shape, jnp.bfloat16) for shape in shapes]
+    small_buffer = pltpu.VMEM((stages,) + small.shape, jnp.float32)
+    return pl.pallas_call(
+        functools.partial(scatter_kernel, orders, expert_size),
+        out_shape=[jax.ShapeDtypeStruct(shape[1:], jnp.float32) for shape in shapes]
+        + [jax.ShapeDtypeStruct(small.shape, jnp.float32)],
+        in_specs=[vmem] * 3,
+        out_specs=[vmem] * 3,
+        scratch_shapes=buffers
+        + buffers
+        + [small_buffer] * 2
+        + [pltpu.SemaphoreType.DMA((3, stages)), pltpu.SemaphoreType.DMA((3, stages))],
+        compiler_params=pltpu.CompilerParams(
+            collective_id=1, has_side_effects=True, vmem_limit_bytes=40 * 2**20
+        ),
+    )(*grads, small)
+
+
+def padded_width(width, rows):
+    unit = 128 if rows % 8 == 0 else 2048
+    return -(-width // unit) * unit
+
+
+def block_shape(rows, width):
+    return (rows, width) if rows % 8 == 0 else (16, rows * width // 16)
+
+
+def widen(array, width):
+    return jnp.pad(array, ((0, 0), (0, width - array.shape[1])))
 
 
 def per_device(
@@ -54,15 +295,35 @@
     owners = lax.axis_size("expert")
     experts = local_experts * owners
     capacity = 5 * length // (4 * experts)
-    gain_one, query_w, key_w, value_w, output_w, router_w, gain_two = (
-        lax.all_gather(gain_attn, ("dp", "expert"), axis=0, tiled=True),
-        lax.all_gather(w_query, ("dp", "expert"), axis=0, tiled=True),
-        lax.all_gather(w_key, ("dp", "expert"), axis=0, tiled=True),
-        lax.all_gather(w_value, ("dp", "expert"), axis=0, tiled=True),
-        lax.all_gather(w_output, ("dp", "expert"), axis=0, tiled=True),
-        lax.all_gather(w_router, ("dp", "expert"), axis=0, tiled=True),
-        lax.all_gather(gain_ffn, ("dp", "expert"), axis=0, tiled=True),
-    )
+    dp_size = lax.axis_size("dp")
+    rows = w_query.shape[0]
+    extras = experts + 2
+    width_one = padded_width(2 * features + extras, rows)
+    width_two = padded_width(2 * features, rows)
+    shard_one = widen(
+        jnp.concatenate(
+            [w_query, w_key, w_router, gain_attn[:, None], gain_ffn[:, None]], axis=1
+        ),
+        width_one,
+    )
+    shard_two = widen(jnp.concatenate([w_value, w_output], axis=1), width_two)
+    whole_one, whole_two = gather_shards(
+        (
+            shard_one.reshape(block_shape(rows, width_one)),
+            shard_two.reshape(block_shape(rows, width_two)),
+        ),
+        dp_size,
+        owners,
+    )
+    whole_one = whole_one.reshape(features, width_one)
+    whole_two = whole_two.reshape(features, width_two)
+    query_w = whole_one[:, :features]
+    key_w = whole_one[:, features : 2 * features]
+    value_w = whole_two[:, :features]
+    output_w = whole_two[:, features : 2 * features]
+    router_w = whole_one[:, 2 * features : 2 * features + experts]
+    gain_one = whole_one[:, 2 * features + experts]
+    gain_two = whole_one[:, 2 * features + experts + 1]
     inputs = tokens.astype(jnp.float32)
     scale_one = lax.rsqrt(jnp.mean(inputs * inputs, axis=-1, keepdims=True) + epsilon)
     unit_one = inputs * scale_one
@@ -113,70 +374,66 @@
     dispatch = (
         position[:, None] == jnp.arange(experts * capacity, dtype=jnp.int32)[None, :]
     ).astype(jnp.bfloat16)
-    slot_shape = (owners, local_experts, capacity, features)
-    outgoing = (
-        jnp.einsum("lc,ld->cd", dispatch, normed_two, preferred_element_type=jnp.float32)
-        .astype(jnp.bfloat16)
-        .reshape(slot_shape)
-    )
-    arrived = lax.all_to_all(outgoing, "expert", split_axis=0, concat_axis=0, tiled=True)
-    pre_act = jnp.einsum("secd,edf->secf", arrived, w_in, preferred_element_type=jnp.float32)
-    hidden_act = gelu_tanh(pre_act).astype(jnp.bfloat16)
-    produced = jnp.einsum(
-        "secf,efd->secd", hidden_act, w_out, preferred_element_type=jnp.float32
-    ).astype(jnp.bfloat16)
-    returned = lax.all_to_all(produced, "expert", split_axis=0, concat_axis=0, tiled=True)
-    combined = jnp.einsum(
-        "lc,cd->ld",
-        dispatch,
-        returned.reshape(experts * capacity, features),
-        preferred_element_type=jnp.float32,
-    )
-    output = residual + gate_prob[:, None] * combined
-    gain_one, query_w, key_w, value_w, output_w, router_w, gain_two = (
-        lax.all_gather(gain_attn, ("dp", "expert"), axis=0, tiled=True),
-        lax.all_gather(w_query, ("dp", "expert"), axis=0, tiled=True),
-        lax.all_gather(w_key, ("dp", "expert"), axis=0, tiled=True),
-        lax.all_gather(w_value, ("dp", "expert"), axis=0, tiled=True),
-        lax.all_gather(w_output, ("dp", "expert"), axis=0, tiled=True),
-        lax.all_gather(w_router, ("dp", "expert"), axis=0, tiled=True),
-        lax.all_gather(gain_ffn, ("dp", "expert"), axis=0, tiled=True),
-    )
     upstream = cotangent.astype(jnp.float32)
     grad_combined = (gate_prob[:, None] * upstream).astype(jnp.bfloat16)
+    slot_shape = (owners, 1, local_experts, capacity, features)
+
+    def to_slots(values):
+        return (
+            jnp.einsum("lc,ld->cd", dispatch, values, preferred_element_type=jnp.float32)
+            .astype(jnp.bfloat16)
+            .reshape(slot_shape)
+        )
+
+    outgoing = jnp.concatenate([to_slots(normed_two), to_slots(grad_combined)], axis=1)
+    both = lax.all_to_all(outgoing, "expert", split_axis=0, concat_axis=0, tiled=True)
+    both_all = lax.all_gather(both, "dp", axis=0, tiled=True)
+    arrived, grad_arrived = (both[:, 0], both[:, 1])
+    rows_all, grads_all = (both_all[:, 0], both_all[:, 1])
+    pre_act = jnp.einsum("secd,edf->secf", arrived, w_in, preferred_element_type=jnp.float32)
+    hidden_act, gelu_pull = jax.vjp(gelu_tanh, pre_act)
+    produced = jnp.einsum(
+        "secf,efd->secd",
+        hidden_act.astype(jnp.bfloat16),
+        w_out,
+        preferred_element_type=jnp.float32,
+    ).astype(jnp.bfloat16)
+    grad_hidden = jnp.einsum(
+        "secd,efd->secf", grad_arrived, w_out, preferred_element_type=jnp.float32
+    )
+    grad_pre = gelu_pull(grad_hidden)[0].astype(jnp.bfloat16)
+    grad_rows = jnp.einsum(
+        "secf,edf->secd", grad_pre, w_in, preferred_element_type=jnp.float32
+    ).astype(jnp.bfloat16)
+    results = jnp.stack([produced, grad_rows], axis=1)
+    returned = lax.all_to_all(results, "expert", split_axis=0, concat_axis=0, tiled=True)
+
+    def from_slots(values):
+        return jnp.einsum(
+            "lc,cd->ld",
+            dispatch,
+            values.reshape(experts * capacity, features),
+            preferred_element_type=jnp.float32,
+        )
+
+    combined = from_slots(returned[:, 0])
+    grad_normed_expert = from_slots(returned[:, 1])
+    output = residual + gate_prob[:, None] * combined
     grad_gate = jnp.sum(upstream * combined, axis=-1)
     grad_logits = (grad_gate * gate_prob)[:, None] * (choose - router_probs)
     grad_router = jnp.dot(normed_two.astype(jnp.float32).T, grad_logits, precision=highest)
     grad_normed_router = jnp.dot(grad_logits, router_w.astype(jnp.float32).T, precision=highest)
-    grad_slots = (
-        jnp.einsum("lc,ld->cd", dispatch, grad_combined, preferred_element_type=jnp.float32)
-        .astype(jnp.bfloat16)
-        .reshape(slot_shape)
-    )
-    grad_arrived = lax.all_to_all(grad_slots, "expert", split_axis=0, concat_axis=0, tiled=True)
-    grad_hidden = jnp.einsum(
-        "secd,efd->secf", grad_arrived, w_out, preferred_element_type=jnp.float32
-    )
-    gelu_value, gelu_pull = jax.vjp(gelu_tanh, pre_act)
-    grad_pre = gelu_pull(grad_hidden)[0].astype(jnp.bfloat16)
-    grad_rows = jnp.einsum(
-        "secf,edf->secd", grad_pre, w_in, preferred_element_type=jnp.float32
-    ).astype(jnp.bfloat16)
-    grad_returned = lax.all_to_all(grad_rows, "expert", split_axis=0, concat_axis=0, tiled=True)
-    grad_normed_expert = jnp.einsum(
-        "lc,cd->ld",
-        dispatch,
-        grad_returned.reshape(experts * capacity, features),
-        preferred_element_type=jnp.float32,
-    )
-    rows_all, grads_all = (
-        lax.all_gather(arrived, "dp", axis=0, tiled=True),
-        lax.all_gather(grad_arrived, "dp", axis=0, tiled=True),
-    )
-    pre_part, act_part = (
-        lax.all_to_all(grad_pre, "dp", split_axis=3, concat_axis=0, tiled=True),
-        lax.all_to_all(hidden_act, "dp", split_axis=3, concat_axis=0, tiled=True),
-    )
+    hidden_part = w_in.shape[2] // dp_size
+    first_hidden = lax.axis_index("dp") * hidden_part
+    in_part = lax.dynamic_slice_in_dim(w_in, first_hidden, hidden_part, axis=2)
+    out_part = lax.dynamic_slice_in_dim(w_out, first_hidden, hidden_part, axis=1)
+    pre_all = jnp.einsum("secd,edf->secf", rows_all, in_part, preferred_element_type=jnp.float32)
+    act_all, pull_all = jax.vjp(gelu_tanh, pre_all)
+    grad_hidden_all = jnp.einsum(
+        "secd,efd->secf", grads_all, out_part, preferred_element_type=jnp.float32
+    )
+    pre_part = pull_all(grad_hidden_all)[0].astype(jnp.bfloat16)
+    act_part = act_all.astype(jnp.bfloat16)
     grad_first_w = jnp.einsum(
         "secd,secf->edf", rows_all, pre_part, preferred_element_type=jnp.float32
     )
@@ -240,27 +497,43 @@
         grad_normed_one, unit_one, scale_one, gain_one.astype(jnp.float32)
     )
     grad_inputs = grad_residual + grad_inner
-    reduced = (
-        lax.psum_scatter(grad_gain_one, ("dp", "expert"), scatter_dimension=0, tiled=True),
-        lax.psum_scatter(grad_query_w, ("dp", "expert"), scatter_dimension=0, tiled=True),
-        lax.psum_scatter(grad_key_w, ("dp", "expert"), scatter_dimension=0, tiled=True),
-        lax.psum_scatter(grad_value_w, ("dp", "expert"), scatter_dimension=0, tiled=True),
-        lax.psum_scatter(grad_output_w, ("dp", "expert"), scatter_dimension=0, tiled=True),
-        lax.psum_scatter(grad_router, ("dp", "expert"), scatter_dimension=0, tiled=True),
-        lax.psum_scatter(grad_gain_two, ("dp", "expert"), scatter_dimension=0, tiled=True),
-    )
-    grad_rel_all = lax.psum(grad_rel, ("dp", "expert"))
+    extra_grads = jnp.concatenate(
+        [grad_router, grad_gain_one[:, None], grad_gain_two[:, None]], axis=1
+    )
+    send_one = widen(
+        jnp.concatenate([grad_query_w, grad_key_w, extra_grads], axis=1).astype(jnp.bfloat16),
+        width_one,
+    )
+    send_two = widen(
+        jnp.concatenate([grad_value_w, grad_output_w], axis=1).astype(jnp.bfloat16), width_two
+    )
+    entries = grad_rel.size
+    small_rows = -(-entries // 1024) * 8
+    small = jnp.pad(grad_rel.reshape(-1), (0, small_rows * 128 - entries))
+    sum_one, sum_two, small_sum = scatter_sums(
+        (
+            send_one.reshape((-1,) + block_shape(rows, width_one)),
+            send_two.reshape((-1,) + block_shape(rows, width_two)),
+        ),
+        small.reshape(small_rows, 128),
+        dp_size,
+        owners,
+    )
+    sum_one = sum_one.reshape(rows, width_one)
+    sum_two = sum_two.reshape(rows, width_two)
+    grad_rel_all = small_sum.reshape(-1)[:entries].reshape(grad_rel.shape)
+    first_extra = 2 * features
     return (
         output.astype(jnp.bfloat16),
         grad_inputs.astype(jnp.bfloat16),
-        reduced[0],
-        reduced[1],
-        reduced[2],
-        reduced[3],
-        reduced[4],
+        sum_one[:, first_extra + experts],
+        sum_one[:, :features],
+        sum_one[:, features : 2 * features],
+        sum_two[:, :features],
+        sum_two[:, features : 2 * features],
         grad_rel_all,
-        reduced[6],
-        reduced[5],
+        sum_one[:, first_extra + experts + 1],
+        sum_one[:, first_extra : first_extra + experts],
         grad_first_w,
         grad_second_w,
     )

time: 738 us -> 299 us (0.41); the launches traced: 728 us -> 297 us
  waiting for transfers between devices: 333 us -> 11.1 us
  blocking collectives: 177 us -> 18.2 us
  Pallas kernels: 0 us -> 95 us
  local copies, waits for them, and re-layouts: 116 us -> 75.2 us
  starting transfers between devices: 28.9 us -> 4.39 us
  other arithmetic: 4.53 us -> 14.9 us
  matrix products: 53.8 us -> 63.9 us
    reduce_scatter x4 -> x0, waiting for transfers between devices: 215 us -> none  [the longest x1 105 us: per_device(): lax.psum_scatter(grad_output_w, ('dp', 'expert'), scatter_dimension=0, ti...]
    all_gather x4 -> x1, waiting for transfers between devices: 101 us -> 0.01 us  [per_device(): both_all = lax.all_gather(both, 'dp', axis=0, tiled=True)]
    pallas_call x0 -> x2, Pallas kernels: none -> 95 us  [the longest x1 47.9 us: gather_shards(): pl.pallas_call(functools.partial(gather_kernel, orders, expert_size), out...]
    unnamed x2 -> x0, blocking collectives: 88.5 us -> none
    all_gather x3 -> x0, blocking collectives: 88.2 us -> none  [the longest x1 66.2 us: per_device(): lax.all_gather(w_router, ('dp', 'expert'), axis=0, tiled=True)]
    unnamed x121 -> x99, local copies, waits for them, and re-layouts: 74 us -> 18.5 us
    all_to_all x6 -> x1, starting transfers between devices: 28.2 us -> 4.13 us  [per_device(): lax.all_to_all(results, 'expert', split_axis=0, concat_axis=0, tiled=True)]
    all_to_all x0 -> x1, blocking collectives: none -> 18.2 us  [per_device(): lax.all_to_all(outgoing, 'expert', split_axis=0, concat_axis=0, tiled=True)]
  transfers between devices with their start and end apart: 14 -> 2, of which waited for: 7 -> 1; matrix products, arithmetic and copies ran while one was open for 22% -> 23% of each run, Pallas kernels for 0% -> 16%
where the time goes in v1:
time: 299 us; the launch traced here: 297 us
  Pallas kernels  95 us (32%)
  local copies, waits for them, and re-layouts  75.2 us (25%)
  matrix products  63.9 us (21%)
  blocking collectives  18.2 us (6%)
  other arithmetic  14.9 us (5%)
  between operations  14.7 us (5%)
  waiting for transfers between devices  11.1 us (4%)
  starting transfers between devices  4.39 us (1%)
    pallas_call x1, Pallas kernels, gather_shards(): pl.pallas_call(functools.partial(gather_kernel, orders, expert_size), out...  47.9 us
    pallas_call x1, Pallas kernels, scatter_sums(): pl.pallas_call(functools.partial(scatter_kernel, orders, expert_size), ou...  47.1 us
    unnamed x99, local copies, waits for them, and re-layouts  18.5 us
    all_to_all x1, blocking collectives, per_device(): lax.all_to_all(outgoing, 'expert', split_axis=0, concat_axis=0, tiled=True)  18.2 us
    all_to_all x1, waiting for transfers between devices, per_device(): lax.all_to_all(results, 'expert', split_axis=0, concat_axis=0, tiled=True)  11.1 us
    concatenate x1, local copies, waits for them, and re-layouts, per_device(): jnp.concatenate([grad_query_w, grad_key_w, extra_grads], axis=1)  9.35 us
    dot_general x1, matrix products, per_device(): jnp.einsum('secf,edf->secd', grad_pre, w_in, preferred_element_type=jnp.f...  8.84 us
    reshape x2, local copies, waits for them, and re-layouts, bias_table(): repeated.reshape(per_offset.shape[0], length, offsets)  8.79 us
  transfers between devices with their start and end apart: 2, of which 1 were waited for; matrix products, arithmetic and copies ran while one was open for 23% of the time, Pallas kernels for 16%

profile of v1, /device:TPU:0, one launch (start us, length us, event | category | flops | bytes accessed | tf_op | source)
XLA Modules:
  0.0 297.4 jit_solution(13367903042845898968)
XLA Ops:
  9.5 0.9 concatenate.21
  11.2 47.9 %shard_map.238 = (bf16[32,24,1664]{2,1,0:T(8,128)(2,1)S(1)}, bf16[32,24,1536]{2,1,0:T(8,128)(2,1)S(1)}) custom-call(bf16[24,1664]{1,0:T(8,128)(2,1)S(1)} %pad.19.refs_0_, bf16[24,1536]{1,0:T(8,128)(2,1)S(1)} %pad_maximum_fusion.3.refs_1_), custom_call_target="tpu_custom_call" | custom-call | tf_op jit(solution)/shard_map/pallas_call | solution.py:142
  59.1 1.5 copy-done.2
  60.6 0.8 fusion.166
  61.6 1.0 fusion.100
  62.6 2.4 convolution_convert_fusion.12
  65.1 2.3 convolution_convert_fusion.11
  69.2 1.2 copy.128
  70.5 1.4 slice.97
  71.9 4.9 %reshape.251 = f32[12,128,255]{2,1,0:T(8,128)} reshape(f32[12,32640]{1,0:T(8,128)} %slice.97) | data formatting | bytes 3133440 | tf_op jit(solution)/shard_map/reshape | solution.py:27
  76.8 1.7 slice.98
  78.5 1.2 copy.122
  79.7 1.1 copy.85
  80.8 1.8 copy.86
  82.7 1.6 fusion.170
  85.0 1.2 convolution_convert_fusion.10
  86.9 1.1 multiply_reduce_fusion.3
  88.5 1.0 copy.123
  90.0 1.1 multiply_convert_fusion.2
  91.1 1.1 fusion.171
  93.7 1.0 convolution_convert_fusion.5
  94.7 2.0 convolution_convert_fusion.4
  96.7 1.7 reshape.254
  98.4 1.7 reshape.253
  100.1 1.1 pad_maximum_fusion.1
  101.7 18.2 %all_to_all.10 = bf16[8,2,1,20,768]{4,1,3,2,0:T(2,128)(2,1)S(1)} all-to-all(bf16[8,2,1,20,768]{4,1,3,2,0:T(2,128)(2,1)S(1)} %copy.92), channel_id=1, replica_groups=mesh['dp'=4,'expert'=8] {'expert'}, dimensions={0} | all-to-all | bytes 983040 | tf_op jit(solution)/shard_map/all_to_all | solution.py:389
  120.7 1.5 fusion.167
  122.2 3.4 %fusion.8 = f32[8,1,20,3072]{3,2,0,1:T(8,128)S(1)} fusion(bf16[1,768,3072]{2,1,0:T(8,128)(2,1)} %param.27, bf16[8,1,1,20,768]{4,1,3,2,0:T(2,128)(2,1)S(1)} %get-tuple-element.71), kind=kOutput, calls=%fused_computation.8 | convolution fusion | flops 754974720 | bytes 6930432 | tf_op jit(solution)/shard_map/secd,edf->secf/dot_general | solution.py:393
  125.6 5.6 %fusion.57 = bf16[8,1,1,20,768]{4,3,0,2,1:T(8,128)(2,1)} fusion(bf16[1,3072,768]{2,1,0:T(8,128)(2,1)} %param.28, f32[8,1,20,3072]{3,2,0,1:T(8,128)S(1)} %fusion.8), kind=kOutput, calls=%fused_computation.65 | convolution fusion | flops 759521280 | bytes 6930432 | tf_op jit(solution)/shard_map/secf,efd->secd/dot_general | solution.py:395
  131.2 8.8 %fusion.62 = bf16[8,1,1,20,768]{4,3,0,2,1:T(8,128)(2,1)} fusion(bf16[1,768,3072]{2,1,0:T(8,128)(2,1)} %param.27, f32[8,1,20,3072]{3,2,0,1:T(8,128)} %copy-done.11, bf16[1,3072,768]{2,1,0:T(8,128)(2,1)} %param.28, bf16[8,1,1,20,768]{4,1,3,2,0:T(2,128)(2,1)} %get-tuple-element.70), kind=kOutput, calls=%fused_computation.74 | convolution fusion | flops 1519902720 | bytes 11894784 | tf_op jit(solution)/shard_map/secf,edf->secd/dot_general | solution.py:405
  140.0 1.1 pad_maximum_fusion.2
  141.2 1.3 copy.95
  142.4 4.1 %all-to-all-start.1 = ((bf16[8,2,1,20,768]{4,1,3,2,0:T(2,128)(2,1)}), bf16[8,2,1,20,768]{4,1,3,2,0:T(2,128)(2,1)}, u32[]{:S(2)}, u32[]{:S(2)}) async-start(bf16[8,2,1,20,768]{4,1,3,2,0:T(2,128)(2,1)} %copy.95), calls=%async_computation.1 | async-start | bytes 983040 | tf_op jit(solution)/shard_map/all_to_all | solution.py:409
  147.6 1.9 copy.105
  149.5 11.1 %all-to-all-done.1 = bf16[8,2,1,20,768]{4,1,3,2,0:T(2,128)(2,1)} async-done(((bf16[8,2,1,20,768]{4,1,3,2,0:T(2,128)(2,1)}), bf16[8,2,1,20,768]{4,1,3,2,0:T(2,128)(2,1)}, u32[]{:S(2)}, u32[]{:S(2)}) %all-to-all-start.1) | async-done | bytes 491552 | tf_op jit(solution)/shard_map/all_to_all | solution.py:409
  160.6 4.1 %slice_reduce_fusion.1 = (bf16[8,20,768]{2,1,0:T(8,128)(2,1)}, bf16[8,20,768]{2,1,0:T(8,128)(2,1)}) fusion(bf16[8,2,1,20,768]{4,1,3,2,0:T(2,128)(2,1)} %all-to-all-done.1), kind=kLoop, calls=%fused_computation.116 | loop fusion | bytes 983040 | tf_op jit(solution)/shard_map/slice | solution.py:420
  164.7 1.7 reshape_squeeze.6
  166.4 2.1 fusion.102
  169.7 2.1 fusion.110
  171.8 1.7 reshape_squeeze.7
  173.5 2.3 multiply_reduce_fusion.1
  175.8 2.1 convert_add_fusion
  178.6 1.2 convolution_convert_fusion.9
  179.8 1.7 copy.96
  181.6 1.4 multiply_reduce_fusion
  184.3 1.1 copy-done.3
  187.9 1.4 fusion.99
  189.2 1.2 copy.127
  191.1 0.9 convolution_convert_fusion.14
  192.0 1.6 convolution_convert_fusion.1
  193.5 1.5 convolution_convert_fusion
  195.1 9.4 %concatenate.25 = bf16[768,1546]{0,1:T(8,128)(2,1)S(1)} concatenate(bf16[768,768]{0,1:T(8,128)(2,1)} %convolution_convert_fusion.1, bf16[768,768]{0,1:T(8,128)(2,1)} %convolution_convert_fusion, bf16[768,8]{0,1:T(8,128)(2,1)S(1)} %convolution_convert_fusion.14, bf16[768,1]{0,1:T(2,128)(2,1)S(1)} %broadcast_in_dim.30, bf16[768,1]{0,1:T(2,128)(2,1)S(1)} %broadcast_in_dim.31), dimensions={1} | concatenate | bytes 4749312 | tf_op jit(solution)/shard_map/concatenate | solution.py:504
  204.4 3.9 %copy.126 = bf16[768,1546]{1,0:T(8,128)(2,1)} copy(bf16[768,1546]{0,1:T(8,128)(2,1)S(1)} %concatenate.25) | data formatting | bytes 4749312
  208.4 2.0 pad.20.clone
  211.1 2.7 pad.21.clone
  213.9 3.9 %reshape.266 = f32[12,32640]{1,0:T(8,128)} reshape(f32[12,128,255]{2,1,0:T(8,128)} %pad.21.clone) | data formatting | bytes 3133440 | tf_op jit(solution)/shard_map/transpose(jvp())/reshape | solution.py:27
  217.7 1.7 pad.22
  220.3 0.9 fusion.118
  222.0 1.4 convolution_convert_fusion.3
  224.1 47.1 %shard_map.239 = (f32[24,1664]{1,0:T(8,128)S(1)}, f32[24,1536]{1,0:T(8,128)S(1)}, f32[8,128]{1,0:T(8,128)S(1)}) custom-call(bf16[32,24,1664]{2,1,0:T(8,128)(2,1)S(1)} %bitcast.227, bf16[32,24,1536]{2,1,0:T(8,128)(2,1)S(1)} %pad_maximum_fusion.refs_1_, f32[8,128]{1,0:T(8,128)S(1)} %pad_bitcast_fusion.refs_2_), custom_call_target="tpu_custom_call" | custom-call | tf_op jit(solution)/shard_map/pallas_call | solution.py:245
  274.2 2.0 fusion.98
  276.2 3.9 %fusion.46 = f32[768,32,20]{0,1,2:T(8,128)} fusion(bf16[1,768,3072]{2,1,0:T(8,128)(2,1)} %param.27, s32[]{:T(128)S(6)} %select_n.10, bf16[32,2,1,20,768]{4,0,3,2,1:T(8,128)(2,1)} %all-gather.2.cloned.1.call-done), kind=kOutput, calls=%fused_computation.56 | convolution fusion | flops 754974720 | bytes 4128772 | tf_op jit(solution)/shard_map/secd,edf->secf/dot_general | solution.py:430
  280.1 6.1 %convolution_bitcast_fusion.1 = f32[1,768,768]{2,1,0:T(8,128)} fusion(f32[768,32,20]{0,1,2:T(8,128)} %fusion.46, bf16[1,3072,768]{2,1,0:T(8,128)(2,1)} %param.28, s32[]{:T(128)S(6)} %select_n.10, bf16[32,2,1,20,768]{4,0,3,2,1:T(8,128)(2,1)S(1)} %copy-done.41), kind=kOutput, calls=%fused_computation.39 | convolution fusion | flops 1519779840 | bytes 7471108 | tf_op jit(solution)/shard_map/secd,secf->edf/dot_general | solution.py:437
  286.2 4.3 %convolution_bitcast_fusion = f32[1,768,768]{2,1,0:T(8,128)} fusion(f32[768,32,20]{0,1,2:T(8,128)} %fusion.46, bf16[32,2,1,20,768]{4,0,3,2,1:T(8,128)(2,1)S(1)} %copy-done.41), kind=kOutput, calls=%fused_computation.38 | convolution fusion | flops 759398400 | bytes 5308416 | tf_op jit(solution)/shard_map/secf,secd->efd/dot_general | solution.py:440
  (142 shorter events, 23.3 us)
Async XLA Ops:
  7.2 61.4 %copy-start = (f32[32,12]{0,1:T(8,128)S(1)}, f32[32,12]{0,1:T(8,128)}, u32[]{:S(2)}) copy-start(f32[32,12]{0,1:T(8,128)} %param.24) | copy-start | bytes 4612
  7.2 57.9 %copy-start.7 = (bf16[128,768]{1,0:T(8,128)(2,1)S(1)}, bf16[128,768]{1,0:T(8,128)(2,1)}, u32[]{:S(2)}) copy-start(bf16[128,768]{1,0:T(8,128)(2,1)} %param.15) | copy-start | bytes 589828
  59.1 1.5 copy-start.2
  62.6 5.2 %copy-start.30 = (f32[128]{0:T(128)}, f32[128]{0:T(128)S(1)}, u32[]{:S(2)}) copy-start(f32[128]{0:T(128)S(1)} %add_rsqrt_fusion.1) | copy-start | bytes 1540
  65.0 3.6 %copy-start.42 = (s32[255]{0:T(256)S(1)}, s32[255]{0:T(256)}, u32[]{:S(2)}) copy-start(s32[255]{0:T(256)} %param.18) | copy-start | bytes 3064
  76.8 5.8 %copy-start.39 = (s32[1,128]{1,0:T(1,128)S(1)}, s32[1,128]{1,0:T(1,128)}, u32[]{:S(2)}) copy-start(s32[1,128]{1,0:T(1,128)} %param.16) | copy-start | bytes 1540
  80.8 5.5 %copy-start.18 = (bf16[128,768]{0,1:T(8,128)(2,1)}, bf16[128,768]{0,1:T(8,128)(2,1)S(1)}, u32[]{:S(2)}) copy-start(bf16[128,768]{0,1:T(8,128)(2,1)S(1)} %copy.85) | copy-start | bytes 589828
  84.3 3.8 %copy-start.25 = (f32[12,128]{1,0:T(8,128)}, f32[12,128]{1,0:T(8,128)S(1)}, u32[]{:S(2)}) copy-start(f32[12,128]{1,0:T(8,128)S(1)} %get-tuple-element.79) | copy-start | bytes 18436
  84.4 0.6 copy-start.27
  85.0 4.6 %copy-start.34 = (s32[128,1]{0,1:T(1,128)S(1)}, s32[128,1]{0,1:T(1,128)}, u32[]{:S(2)}) copy-start(s32[128,1]{0,1:T(1,128)} %param.17) | copy-start | bytes 1540
  86.2 0.7 copy-start.22
  89.6 12.1 %copy-start.26 = (f32[768]{0:T(1024)}, f32[768]{0:T(1024)S(1)}, u32[]{:S(2)}) copy-start(f32[768]{0:T(1024)S(1)} %convert_reduce_fusion) | copy-start | bytes 9220
  92.2 0.8 copy-start.28
  92.3 0.7 copy-start.35
  93.0 1.7 copy-start.37
  93.7 26.3 %copy-start.36 = (s32[128]{0:T(128)}, s32[128]{0:T(128)S(1)}, u32[]{:S(2)}) copy-start(s32[128]{0:T(128)S(1)} %fusion.134) | copy-start | bytes 1540
  119.9 0.8 copy-start.6
  125.6 5.6 %copy-start.11 = (f32[8,1,20,3072]{3,2,0,1:T(8,128)}, f32[8,1,20,3072]{3,2,0,1:T(8,128)S(1)}, u32[]{:S(2)}) copy-start(f32[8,1,20,3072]{3,2,0,1:T(8,128)S(1)} %fusion.8) | copy-start | bytes 5898244
  142.4 18.2 %all-to-all-start.1 = ((bf16[8,2,1,20,768]{4,1,3,2,0:T(2,128)(2,1)}), bf16[8,2,1,20,768]{4,1,3,2,0:T(2,128)(2,1)}, u32[]{:S(2)}, u32[]{:S(2)}) async-start(bf16[8,2,1,20,768]{4,1,3,2,0:T(2,128)(2,1)} %copy.95), calls=%async_computation.1 | async-start | bytes 983040 | tf_op jit(solution)/shard_map/all_to_all | solution.py:409
  146.6 129.6 %all-gather.2.cloned.1.call-start = ((), (), s32[]{:S(2)}) async-start(), calls=%async_computation.2 | async-start | bytes 2457600 | tf_op jit(solution)/shard_map/all_gather | solution.py:390
  169.2 0.5 copy-start.38
  177.9 0.7 copy-start.8
  181.6 1.6 copy-start.20
  181.6 1.9 copy-start.19
  183.0 0.9 copy-start.21
  183.2 2.8 copy-start.4
  183.2 2.2 copy-start.3
  183.4 3.1 %copy-start.14 = (bf16[12,64,128]{2,1,0:T(8,128)(2,1)}, bf16[12,64,128]{2,1,0:T(8,128)(2,1)S(1)}, u32[]{:S(2)}) copy-start(bf16[12,64,128]{2,1,0:T(8,128)(2,1)S(1)} %convolution_convert_fusion.8) | copy-start | bytes 589828
  183.9 2.6 copy-start.16
  184.3 2.8 copy-start.12
  186.0 1.9 copy-start.31
  186.0 3.3 %copy-start.5 = (f32[12,128,128]{1,2,0:T(8,128)S(1)}, f32[12,128,128]{1,2,0:T(8,128)}, u32[]{:S(2)}) copy-start(f32[12,128,128]{1,2,0:T(8,128)} %copy-done.4) | copy-start | bytes 2359300
  186.5 4.6 %copy-start.29 = (f32[128]{0:T(128)S(1)}, f32[128]{0:T(128)}, u32[]{:S(2)}) copy-start(f32[128]{0:T(128)} %copy-done.28) | copy-start | bytes 1540
  187.1 0.8 copy-start.10
  187.8 4.1 %copy-start.15 = (bf16[12,64,128]{2,1,0:T(8,128)(2,1)S(1)}, bf16[12,64,128]{2,1,0:T(8,128)(2,1)}, u32[]{:S(2)}) copy-start(bf16[12,64,128]{2,1,0:T(8,128)(2,1)} %copy-done.14) | copy-start | bytes 589828
  187.8 4.1 %copy-start.32 = (f32[128]{0:T(128)S(1)}, f32[128]{0:T(128)}, u32[]{:S(2)}) copy-start(f32[128]{0:T(128)} %copy-done.30) | copy-start | bytes 1540
  187.8 5.7 %copy-start.17 = (bf16[12,64,128]{2,1,0:T(8,128)(2,1)S(1)}, bf16[12,64,128]{2,1,0:T(8,128)(2,1)}, u32[]{:S(2)}) copy-start(bf16[12,64,128]{2,1,0:T(8,128)(2,1)} %copy-done.16) | copy-start | bytes 589828
  208.4 2.0 copy-start.24
  219.5 0.8 copy-start.43
  219.5 2.5 copy-start.13
  220.1 3.3 %copy-start.9 = (f32[128,768]{1,0:T(8,128)S(1)}, f32[128,768]{1,0:T(8,128)}, u32[]{:S(2)}) copy-start(f32[128,768]{1,0:T(8,128)} %copy-done.8) | copy-start | bytes 1179652
  220.1 3.3 %copy-start.23 = (bf16[12,64,128]{2,1,0:T(8,128)(2,1)S(1)}, bf16[12,64,128]{2,1,0:T(8,128)(2,1)}, u32[]{:S(2)}) copy-start(bf16[12,64,128]{2,1,0:T(8,128)(2,1)} %copy-done.22) | copy-start | bytes 589828
  224.1 49.3 %copy-start.40 = (f32[128]{0:T(128)S(1)}, f32[128]{0:T(128)}, u32[]{:S(2)}) copy-start(f32[128]{0:T(128)} %get-tuple-element.61) | copy-start | bytes 1540
  224.1 50.0 %copy-start.33 = (f32[128]{0:T(128)S(1)}, f32[128]{0:T(128)}, u32[]{:S(2)}) copy-start(f32[128]{0:T(128)} %copy-done.30) | copy-start | bytes 1540
  276.2 3.9 %copy-start.41 = (bf16[32,2,1,20,768]{4,0,3,2,1:T(8,128)(2,1)S(1)}, bf16[32,2,1,20,768]{4,0,3,2,1:T(8,128)(2,1)}, u32[]{:S(2)}) copy-start(bf16[32,2,1,20,768]{4,0,3,2,1:T(8,128)(2,1)} %all-gather.2.cloned.1.call-done) | copy-start | bytes 5898244
  286.2 4.3 %copy-start.1 = (f32[32,12]{0,1:T(8,128)S(1)}, f32[32,12]{0,1:T(8,128)}, u32[]{:S(2)}) copy-start(f32[32,12]{0,1:T(8,128)} %param.24) | copy-start | bytes 4612
Sparse Core Ops, SparseCore 0:
  149.6 21.9 all-gather.1

commit v2 on v1

--- a/solution.py
+++ b/solution.py
@@ -15,23 +15,10 @@
     return jax.nn.gelu(values, approximate=True)
 
 
-def bias_table(rel_bias, bucket_table):
-    offsets = bucket_table.shape[0]
-    length = (offsets + 1) // 2
-    onehot = (
-        bucket_table[:, None] == jnp.arange(rel_bias.shape[0], dtype=jnp.int32)[None, :]
+def offset_onehot(bucket_table, buckets):
+    return (
+        bucket_table[:, None] == jnp.arange(buckets, dtype=jnp.int32)[None, :]
     ).astype(jnp.float32)
-    per_offset = jnp.dot(onehot, rel_bias, precision=highest).T
-    padded = jnp.concatenate([per_offset, jnp.zeros((per_offset.shape[0], 1), jnp.float32)], axis=1)
-    repeated = jnp.tile(padded, (1, length))[:, : length * offsets]
-    return repeated.reshape(per_offset.shape[0], length, offsets)[:, :, length - 1 : offsets]
-
-
-def norm_back(grad_normed, unit, scale, gain):
-    grad_unit = grad_normed * gain
-    grad_gain = jnp.sum(grad_normed * unit, axis=0)
-    grad_input = scale * (grad_unit - unit * jnp.mean(grad_unit * unit, axis=-1, keepdims=True))
-    return (grad_gain, grad_input)
 
 
 def doubling(count):
@@ -269,6 +256,242 @@
 
 def widen(array, width):
     return jnp.pad(array, ((0, 0), (0, width - array.shape[1])))
+
+
+def contract(left, right, dims, precision=None):
+    return lax.dot_general(
+        left,
+        right,
+        (((dims[0],), (dims[1],)), ((), ())),
+        precision=precision,
+        preferred_element_type=jnp.float32,
+    )
+
+
+def unit_rows(values):
+    scale = lax.rsqrt(jnp.mean(values * values, axis=-1, keepdims=True) + epsilon)
+    return (scale, values * scale)
+
+
+def gain_rows(one_ref, features, experts):
+    turned = one_ref[:, 2 * features : 2 * features + 128].astype(jnp.float32).T
+    return (turned[experts : experts + 1], turned[experts + 1 : experts + 2])
+
+
+def forward_kernel(
+    experts,
+    capacity,
+    heads,
+    tokens,
+    segment_col,
+    segment_row,
+    routes,
+    table,
+    one_ref,
+    two_ref,
+    cotangent,
+    normed_ref,
+    query_ref,
+    keyed_ref,
+    valued_ref,
+    probs_ref,
+    attended_ref,
+    residual_ref,
+    normed_two_ref,
+    router_ref,
+    dispatch_ref,
+    slots_ref,
+):
+    length, features = tokens.shape
+    size = features // heads
+    inputs = tokens[...].astype(jnp.float32)
+    gain_one, gain_two = gain_rows(one_ref, features, experts)
+    normed = (unit_rows(inputs)[1] * gain_one).astype(jnp.bfloat16)
+    normed_ref[...] = normed
+    query_ref[...] = contract(normed, one_ref[:, :features], (1, 0)).astype(jnp.bfloat16)
+    keyed_ref[...] = contract(normed, one_ref[:, features : 2 * features], (1, 0)).astype(
+        jnp.bfloat16
+    )
+    valued_ref[...] = contract(normed, two_ref[:, :features], (1, 0)).astype(jnp.bfloat16)
+    same_doc = segment_col[...] == segment_row[...]
+    for head in range(heads):
+        span = slice(head * size, (head + 1) * size)
+        spread = jnp.broadcast_to(table[head : head + 1, :], (length, 2 * length))
+        bias = pltpu.roll(spread, length + 1, 1, stride=1, stride_axis=0)[:, :length]
+        scores = contract(query_ref[:, span], keyed_ref[:, span], (1, 1)) + bias
+        scores = jnp.where(same_doc, scores, -1e30)
+        powers = jnp.exp(scores - jnp.max(scores, axis=-1, keepdims=True))
+        probs = powers / jnp.sum(powers, axis=-1, keepdims=True)
+        probs_ref[head] = probs
+        attended_ref[:, span] = contract(
+            probs.astype(jnp.bfloat16), valued_ref[:, span], (1, 0)
+        ).astype(jnp.bfloat16)
+    residual = inputs + contract(attended_ref[...], two_ref[:, features : 2 * features], (1, 0))
+    residual_ref[...] = residual
+    normed_two = (unit_rows(residual)[1] * gain_two).astype(jnp.bfloat16)
+    normed_two_ref[...] = normed_two
+    lanes = lax.broadcasted_iota(jnp.int32, (length, 128), 1)
+    logits = contract(normed_two, one_ref[:, 2 * features : 2 * features + 128], (1, 0))
+    logits = jnp.where(lanes < experts, logits, -1e30)
+    powers = jnp.exp(logits - jnp.max(logits, axis=-1, keepdims=True))
+    router = powers / jnp.sum(powers, axis=-1, keepdims=True)
+    router_ref[...] = router
+    choose = (routes[...] == lanes).astype(jnp.float32)
+    gate = jnp.sum(router * choose, axis=-1, keepdims=True)
+    rows = lax.broadcasted_iota(jnp.int32, (length, length), 0)
+    columns = lax.broadcasted_iota(jnp.int32, (length, length), 1)
+    below = (columns < rows).astype(jnp.float32).astype(jnp.bfloat16)
+    earlier = contract(below, choose.astype(jnp.bfloat16), (1, 0))
+    position = jnp.sum(earlier * choose, axis=-1, keepdims=True).astype(jnp.int32)
+    position = position + routes[...] * (2 * capacity)
+    places = lax.broadcasted_iota(jnp.int32, (length, 2 * experts * capacity), 1)
+    token_place = (places == position).astype(jnp.float32)
+    grad_place = (places == position + capacity).astype(jnp.float32)
+    dispatch = jnp.concatenate([token_place, grad_place], axis=0).astype(jnp.bfloat16)
+    dispatch_ref[...] = dispatch
+    weighted = (gate * cotangent[...].astype(jnp.float32)).astype(jnp.bfloat16)
+    slots_ref[...] = contract(
+        dispatch, jnp.concatenate([normed_two, weighted], axis=0), (0, 0)
+    ).astype(jnp.bfloat16)
+
+
+def backward_kernel(
+    experts,
+    heads,
+    tokens,
+    routes,
+    one_ref,
+    two_ref,
+    cotangent,
+    normed_ref,
+    query_ref,
+    keyed_ref,
+    valued_ref,
+    probs_ref,
+    attended_ref,
+    residual_ref,
+    normed_two_ref,
+    router_ref,
+    dispatch_ref,
+    returned_ref,
+    output_ref,
+    grad_tokens_ref,
+    grad_one_ref,
+    grad_two_ref,
+    offsets_ref,
+    grad_query_ref,
+    grad_key_ref,
+    grad_value_ref,
+):
+    length, features = tokens.shape
+    size = features // heads
+    last = 2 * features
+    gain_one, gain_two = gain_rows(one_ref, features, experts)
+    scale_one, unit_one = unit_rows(tokens[...].astype(jnp.float32))
+    residual = residual_ref[...]
+    scale_two, unit_two = unit_rows(residual)
+    upstream = cotangent[...].astype(jnp.float32)
+    both = contract(dispatch_ref[...], returned_ref[...], (1, 0))
+    combined = both[:length]
+    lanes = lax.broadcasted_iota(jnp.int32, (length, 128), 1)
+    choose = (routes[...] == lanes).astype(jnp.float32)
+    router = router_ref[...]
+    gate = jnp.sum(router * choose, axis=-1, keepdims=True)
+    output_ref[...] = (residual + gate * combined).astype(jnp.bfloat16)
+    grad_gate = jnp.sum(upstream * combined, axis=-1, keepdims=True)
+    grad_logits = grad_gate * gate * (choose - router)
+    router_w = one_ref[:, last : last + 128].astype(jnp.float32)
+    grad_normed_two = both[length:] + contract(grad_logits, router_w, (1, 1), highest)
+    grad_unit = grad_normed_two * gain_two
+    grad_residual = upstream + scale_two * (
+        grad_unit - unit_two * jnp.mean(grad_unit * unit_two, axis=-1, keepdims=True)
+    )
+    grad_attn = grad_residual.astype(jnp.bfloat16)
+    grad_two_ref[:, features:last] = contract(attended_ref[...], grad_attn, (0, 0)).astype(
+        jnp.bfloat16
+    )
+    grad_attended = contract(grad_attn, two_ref[:, features:last], (1, 1)).astype(jnp.bfloat16)
+    rows = lax.broadcasted_iota(jnp.int32, (length, length), 0)
+    columns = lax.broadcasted_iota(jnp.int32, (length, length), 1)
+    turn = (rows + columns == length - 1).astype(jnp.float32)
+    for head in range(heads):
+        span = slice(head * size, (head + 1) * size)
+        probs = probs_ref[head]
+        grad_head = grad_attended[:, span]
+        grad_value_ref[:, span] = contract(probs.astype(jnp.bfloat16), grad_head, (0, 0)).astype(
+            jnp.bfloat16
+        )
+        grad_probs = contract(grad_head, valued_ref[:, span], (1, 1))
+        grad_scores = probs * (grad_probs - jnp.sum(grad_probs * probs, axis=-1, keepdims=True))
+        turned = contract(turn, grad_scores, (1, 0), highest)
+        spread = jnp.concatenate([turned, jnp.zeros_like(turned)], axis=1)
+        spread = pltpu.roll(spread, 0, 1, stride=1, stride_axis=0)
+        offsets_ref[head : head + 1, :] = jnp.sum(spread, axis=0, keepdims=True)
+        scores_low = grad_scores.astype(jnp.bfloat16)
+        grad_query_ref[:, span] = contract(scores_low, keyed_ref[:, span], (1, 0)).astype(
+            jnp.bfloat16
+        )
+        grad_key_ref[:, span] = contract(scores_low, query_ref[:, span], (0, 0)).astype(
+            jnp.bfloat16
+        )
+    normed = normed_ref[...]
+    grad_query, grad_key, grad_value = (
+        grad_query_ref[...],
+        grad_key_ref[...],
+        grad_value_ref[...],
+    )
+    grad_one_ref[:, :features] = contract(normed, grad_query, (0, 0)).astype(jnp.bfloat16)
+    grad_one_ref[:, features:last] = contract(normed, grad_key, (0, 0)).astype(jnp.bfloat16)
+    grad_two_ref[:, :features] = contract(normed, grad_value, (0, 0)).astype(jnp.bfloat16)
+    grad_normed = contract(grad_query, one_ref[:, :features], (1, 1))
+    grad_normed = grad_normed + contract(grad_key, one_ref[:, features:last], (1, 1))
+    grad_normed = grad_normed + contract(grad_value, two_ref[:, :features], (1, 1))
+    grad_unit = grad_normed * gain_one
+    grad_tokens_ref[...] = (
+        grad_residual
+        + scale_one
+        * (grad_unit - unit_one * jnp.mean(grad_unit * unit_one, axis=-1, keepdims=True))
+    ).astype(jnp.bfloat16)
+    left = jnp.concatenate(
+        [
+            normed_two_ref[...].astype(jnp.float32),
+            grad_normed * unit_one,
+            grad_normed_two * unit_two,
+        ],
+        axis=0,
+    )
+    right = jnp.concatenate(
+        [
+            grad_logits,
+            (lanes == experts).astype(jnp.float32),
+            (lanes == experts + 1).astype(jnp.float32),
+        ],
+        axis=0,
+    )
+    grad_one_ref[:, last : last + 128] = contract(left, right, (0, 0), highest).astype(
+        jnp.bfloat16
+    )
+    if grad_one_ref.shape[1] > last + 128:
+        rest = grad_one_ref.shape[1] - last - 128
+        grad_one_ref[:, last + 128 :] = jnp.zeros((features, rest), jnp.bfloat16)
+    if grad_two_ref.shape[1] > last:
+        rest = grad_two_ref.shape[1] - last
+        grad_two_ref[:, last:] = jnp.zeros((features, rest), jnp.bfloat16)
+
+
+def local_call(kernel, inputs, outputs, scratch=(), flops=0):
+    vmem = pl.BlockSpec(memory_space=pltpu.VMEM)
+    return pl.pallas_call(
+        kernel,
+        out_shape=[jax.ShapeDtypeStruct(shape, dtype) for shape, dtype in outputs],
+        in_specs=[vmem] * len(inputs),
+        out_specs=[vmem] * len(outputs),
+        scratch_shapes=list(scratch),
+        compiler_params=pltpu.CompilerParams(vmem_limit_bytes=50 * 2**20),
+        cost_estimate=pl.CostEstimate(
+            flops=flops, bytes_accessed=12 * 10**6, transcendentals=200000
+        ),
+    )(*inputs)
 
 
 def per_device(
@@ -317,79 +540,42 @@
     )
     whole_one = whole_one.reshape(features, width_one)
     whole_two = whole_two.reshape(features, width_two)
-    query_w = whole_one[:, :features]
-    key_w = whole_one[:, features : 2 * features]
-    value_w = whole_two[:, :features]
-    output_w = whole_two[:, features : 2 * features]
-    router_w = whole_one[:, 2 * features : 2 * features + experts]
-    gain_one = whole_one[:, 2 * features + experts]
-    gain_two = whole_one[:, 2 * features + experts + 1]
-    inputs = tokens.astype(jnp.float32)
-    scale_one = lax.rsqrt(jnp.mean(inputs * inputs, axis=-1, keepdims=True) + epsilon)
-    unit_one = inputs * scale_one
-    normed = (unit_one * gain_one.astype(jnp.float32)).astype(jnp.bfloat16)
-    query = (
-        jnp.dot(normed, query_w, preferred_element_type=jnp.float32)
-        .astype(jnp.bfloat16)
-        .reshape(length, num_heads, head_size)
-    )
-    keyed = (
-        jnp.dot(normed, key_w, preferred_element_type=jnp.float32)
-        .astype(jnp.bfloat16)
-        .reshape(length, num_heads, head_size)
-    )
-    valued = (
-        jnp.dot(normed, value_w, preferred_element_type=jnp.float32)
-        .astype(jnp.bfloat16)
-        .reshape(length, num_heads, head_size)
-    )
-    pos_bias = bias_table(rel_bias, bucket_table)
-    segment = segment_ids[0]
-    same_doc = segment[:, None] == segment[None, :]
-
-    def scores_of():
-        raw_scores = jnp.einsum("qhe,khe->hqk", query, keyed, preferred_element_type=jnp.float32)
-        return jnp.where(same_doc[None], raw_scores + pos_bias, -1e30)
-
-    scores = scores_of()
-    row_peak = jnp.max(scores, axis=-1, keepdims=True)
-    exp_scores = jnp.exp(scores - row_peak)
-    row_total = jnp.sum(exp_scores, axis=-1, keepdims=True)
-    attn_probs = exp_scores / row_total
-    log_total = row_peak + jnp.log(row_total)
-    attended = jnp.einsum(
-        "hqk,khe->qhe", attn_probs.astype(jnp.bfloat16), valued, preferred_element_type=jnp.float32
-    )
-    attended = attended.astype(jnp.bfloat16).reshape(length, features)
-    residual = inputs + jnp.dot(attended, output_w, preferred_element_type=jnp.float32)
-    scale_two = lax.rsqrt(jnp.mean(residual * residual, axis=-1, keepdims=True) + epsilon)
-    unit_two = residual * scale_two
-    normed_two = (unit_two * gain_two.astype(jnp.float32)).astype(jnp.bfloat16)
-    logits = jnp.dot(normed_two, router_w, preferred_element_type=jnp.float32)
-    router_probs = jax.nn.softmax(logits, axis=-1)
-    choose = (routes == jnp.arange(experts, dtype=jnp.int32)[None, :]).astype(jnp.float32)
-    gate_prob = jnp.sum(router_probs * choose, axis=-1)
-    earlier = jnp.cumsum(choose, axis=0) - choose
-    position = jnp.sum(earlier * choose, axis=-1).astype(jnp.int32) + routes[:, 0] * capacity
-    dispatch = (
-        position[:, None] == jnp.arange(experts * capacity, dtype=jnp.int32)[None, :]
-    ).astype(jnp.bfloat16)
-    upstream = cotangent.astype(jnp.float32)
-    grad_combined = (gate_prob[:, None] * upstream).astype(jnp.bfloat16)
-    slot_shape = (owners, 1, local_experts, capacity, features)
-
-    def to_slots(values):
-        return (
-            jnp.einsum("lc,ld->cd", dispatch, values, preferred_element_type=jnp.float32)
-            .astype(jnp.bfloat16)
-            .reshape(slot_shape)
-        )
-
-    outgoing = jnp.concatenate([to_slots(normed_two), to_slots(grad_combined)], axis=1)
+    onehot = offset_onehot(bucket_table, rel_bias.shape[0])
+    table = jnp.pad(jnp.dot(onehot, rel_bias, precision=highest).T, ((0, 0), (0, 1)))
+    low, full = jnp.bfloat16, jnp.float32
+    dense_flops = 2 * length * features * features
+    saved = local_call(
+        functools.partial(forward_kernel, experts, capacity, num_heads),
+        (
+            tokens,
+            segment_ids.reshape(length, 1),
+            segment_ids,
+            routes,
+            table,
+            whole_one,
+            whole_two,
+            cotangent,
+        ),
+        [
+            ((length, features), low),
+            ((length, features), low),
+            ((length, features), low),
+            ((length, features), low),
+            ((num_heads, length, length), full),
+            ((length, features), low),
+            ((length, features), full),
+            ((length, features), low),
+            ((length, 128), full),
+            ((2 * length, 2 * experts * capacity), low),
+            ((2 * experts * capacity, features), low),
+        ],
+        flops=5 * dense_flops,
+    )
+    outgoing = saved[-1].reshape(owners, local_experts, 2 * capacity, features)
     both = lax.all_to_all(outgoing, "expert", split_axis=0, concat_axis=0, tiled=True)
     both_all = lax.all_gather(both, "dp", axis=0, tiled=True)
-    arrived, grad_arrived = (both[:, 0], both[:, 1])
-    rows_all, grads_all = (both_all[:, 0], both_all[:, 1])
+    arrived, grad_arrived = (both[:, :, :capacity], both[:, :, capacity:])
+    rows_all, grads_all = (both_all[:, :, :capacity], both_all[:, :, capacity:])
     pre_act = jnp.einsum("secd,edf->secf", arrived, w_in, preferred_element_type=jnp.float32)
     hidden_act, gelu_pull = jax.vjp(gelu_tanh, pre_act)
     produced = jnp.einsum(
@@ -405,24 +591,31 @@
     grad_rows = jnp.einsum(
         "secf,edf->secd", grad_pre, w_in, preferred_element_type=jnp.float32
     ).astype(jnp.bfloat16)
-    results = jnp.stack([produced, grad_rows], axis=1)
+    results = jnp.concatenate([produced, grad_rows], axis=2)
     returned = lax.all_to_all(results, "expert", split_axis=0, concat_axis=0, tiled=True)
 
-    def from_slots(values):
-        return jnp.einsum(
-            "lc,cd->ld",
-            dispatch,
-            values.reshape(experts * capacity, features),
-            preferred_element_type=jnp.float32,
-        )
-
-    combined = from_slots(returned[:, 0])
-    grad_normed_expert = from_slots(returned[:, 1])
-    output = residual + gate_prob[:, None] * combined
-    grad_gate = jnp.sum(upstream * combined, axis=-1)
-    grad_logits = (grad_gate * gate_prob)[:, None] * (choose - router_probs)
-    grad_router = jnp.dot(normed_two.astype(jnp.float32).T, grad_logits, precision=highest)
-    grad_normed_router = jnp.dot(grad_logits, router_w.astype(jnp.float32).T, precision=highest)
+    output, grad_inputs, send_one, send_two, grad_offsets = local_call(
+        functools.partial(backward_kernel, experts, num_heads),
+        (
+            tokens,
+            routes,
+            whole_one,
+            whole_two,
+            cotangent,
+            *saved[:-1],
+            returned.reshape(2 * experts * capacity, features),
+        ),
+        [
+            ((length, features), low),
+            ((length, features), low),
+            ((features, width_one), low),
+            ((features, width_two), low),
+            ((num_heads, 2 * length), full),
+        ],
+        scratch=[pltpu.VMEM((length, features), low)] * 3,
+        flops=10 * dense_flops,
+    )
+    grad_rel = jnp.dot(onehot.T, grad_offsets[:, :-1].T, precision=highest)
     hidden_part = w_in.shape[2] // dp_size
     first_hidden = lax.axis_index("dp") * hidden_part
     in_part = lax.dynamic_slice_in_dim(w_in, first_hidden, hidden_part, axis=2)
@@ -440,73 +633,6 @@
     grad_second_w = jnp.einsum(
         "secf,secd->efd", act_part, grads_all, preferred_element_type=jnp.float32
     )
-    grad_normed_two = grad_normed_router + grad_normed_expert
-    grad_gain_two, grad_through = norm_back(
-        grad_normed_two, unit_two, scale_two, gain_two.astype(jnp.float32)
-    )
-    grad_residual = upstream + grad_through
-    grad_attn = grad_residual.astype(jnp.bfloat16)
-    grad_output_w = jnp.einsum("ld,le->de", attended, grad_attn, preferred_element_type=jnp.float32)
-    grad_attended = (
-        jnp.einsum("le,de->ld", grad_attn, output_w, preferred_element_type=jnp.float32)
-        .astype(jnp.bfloat16)
-        .reshape(length, num_heads, head_size)
-    )
-    attn_probs = jnp.exp(scores_of() - log_total)
-    grad_value = jnp.einsum(
-        "hqk,qhe->khe",
-        attn_probs.astype(jnp.bfloat16),
-        grad_attended,
-        preferred_element_type=jnp.float32,
-    ).astype(jnp.bfloat16)
-    grad_probs = jnp.einsum(
-        "qhe,khe->hqk", grad_attended, valued, preferred_element_type=jnp.float32
-    )
-    grad_scores = attn_probs * (
-        grad_probs - jnp.sum(grad_probs * attn_probs, axis=-1, keepdims=True)
-    )
-    bias_value, bias_pull = jax.vjp(
-        lambda table_bias: bias_table(table_bias, bucket_table), rel_bias
-    )
-    grad_rel = bias_pull(grad_scores)[0]
-    scores_low = grad_scores.astype(jnp.bfloat16)
-    grad_query = (
-        jnp.einsum("hqk,khe->qhe", scores_low, keyed, preferred_element_type=jnp.float32)
-        .astype(jnp.bfloat16)
-        .reshape(length, features)
-    )
-    grad_key = (
-        jnp.einsum("hqk,qhe->khe", scores_low, query, preferred_element_type=jnp.float32)
-        .astype(jnp.bfloat16)
-        .reshape(length, features)
-    )
-    grad_value = grad_value.reshape(length, features)
-    grad_query_w = jnp.einsum("ld,le->de", normed, grad_query, preferred_element_type=jnp.float32)
-    grad_key_w = jnp.einsum("ld,le->de", normed, grad_key, preferred_element_type=jnp.float32)
-    grad_value_w = jnp.einsum("ld,le->de", normed, grad_value, preferred_element_type=jnp.float32)
-    grad_normed_one = jnp.einsum(
-        "le,de->ld", grad_query, query_w, preferred_element_type=jnp.float32
-    )
-    grad_normed_one = grad_normed_one + jnp.einsum(
-        "le,de->ld", grad_key, key_w, preferred_element_type=jnp.float32
-    )
-    grad_normed_one = grad_normed_one + jnp.einsum(
-        "le,de->ld", grad_value, value_w, preferred_element_type=jnp.float32
-    )
-    grad_gain_one, grad_inner = norm_back(
-        grad_normed_one, unit_one, scale_one, gain_one.astype(jnp.float32)
-    )
-    grad_inputs = grad_residual + grad_inner
-    extra_grads = jnp.concatenate(
-        [grad_router, grad_gain_one[:, None], grad_gain_two[:, None]], axis=1
-    )
-    send_one = widen(
-        jnp.concatenate([grad_query_w, grad_key_w, extra_grads], axis=1).astype(jnp.bfloat16),
-        width_one,
-    )
-    send_two = widen(
-        jnp.concatenate([grad_value_w, grad_output_w], axis=1).astype(jnp.bfloat16), width_two
-    )
     entries = grad_rel.size
     small_rows = -(-entries // 1024) * 8
     small = jnp.pad(grad_rel.reshape(-1), (0, small_rows * 128 - entries))
@@ -524,8 +650,8 @@
     grad_rel_all = small_sum.reshape(-1)[:entries].reshape(grad_rel.shape)
     first_extra = 2 * features
     return (
-        output.astype(jnp.bfloat16),
-        grad_inputs.astype(jnp.bfloat16),
+        output,
+        grad_inputs,
         sum_one[:, first_extra + experts],
         sum_one[:, :features],
         sum_one[:, features : 2 * features],

time: 299 us -> 225 us (0.75)
  local copies, waits for them, and re-layouts: 75.2 us -> 20 us
  matrix products: 63.9 us -> 34.6 us
  Pallas kernels: 95 us -> 117 us
  other arithmetic: 14.9 us -> 2.72 us
  waiting for transfers between devices: 11.1 us -> 14.1 us
    dot_general x27 -> x2, matrix products: 31.7 us -> 1.15 us  [the longest x1 0.87 us: per_device(): jnp.dot(onehot, rel_bias, precision=highest)]
    pallas_call x0 -> x2, Pallas kernels: none -> 21.4 us  [local_call(): pl.pallas_call(kernel, out_shape=[jax.ShapeDtypeStruct(shape, dtype) for...]
    reshape x4 -> x1, local copies, waits for them, and re-layouts: 12.2 us -> 0.76 us  [per_device(): segment_ids.reshape(length, 1)]
    concatenate x3 -> x0, local copies, waits for them, and re-layouts: 9.93 us -> none  [the longest x1 9.35 us: per_device(): jnp.concatenate([grad_query_w, grad_key_w, extra_grads], axis=1)]
    slice x5 -> x1, local copies, waits for them, and re-layouts: 9.55 us -> 2.08 us  [per_device(): rows_all, grads_all = (both_all[:, :, :capacity], both_all[:, :, capacity:])]
    convert_element_type x5 -> x0, local copies, waits for them, and re-layouts: 5.56 us -> none  [the longest x1 1.81 us: per_device(): keyed = jnp.dot(normed, key_w, preferred_element_type=jnp.float32).astype...]
    unnamed x99 -> x34, local copies, waits for them, and re-layouts: 18.5 us -> 13.1 us
    another operation x5 -> x0, local copies, waits for them, and re-layouts: 4.87 us -> none  [the longest x2 3.42 us: from_slots(): values.reshape(experts * capacity, features)]
  transfers between devices with their start and end apart: 2 -> 2, of which waited for: 1 -> 1; matrix products, arithmetic and copies ran while one was open for 23% -> 9% of each run, Pallas kernels for 16% -> 27%
where the time goes in v2:
time: 225 us; the launch traced here: 224 us
  Pallas kernels  117 us (52%)
  matrix products  34.6 us (15%)
  local copies, waits for them, and re-layouts  20 us (9%)
  blocking collectives  18.2 us (8%)
  between operations  14.2 us (6%)
  waiting for transfers between devices  14.1 us (6%)
  starting transfers between devices  4.05 us (2%)
  other arithmetic  2.72 us (1%)
    pallas_call x1, Pallas kernels, gather_shards(): pl.pallas_call(functools.partial(gather_kernel, orders, expert_size), out...  47.9 us
    pallas_call x1, Pallas kernels, scatter_sums(): pl.pallas_call(functools.partial(scatter_kernel, orders, expert_size), ou...  47.3 us
    pallas_call x2, Pallas kernels, local_call(): pl.pallas_call(kernel, out_shape=[jax.ShapeDtypeStruct(shape, dtype) for...  21.4 us
    all_to_all x1, blocking collectives, per_device(): lax.all_to_all(outgoing, 'expert', split_axis=0, concat_axis=0, tiled=True)  18.2 us
    all_to_all x1, waiting for transfers between devices, per_device(): lax.all_to_all(results, 'expert', split_axis=0, concat_axis=0, tiled=True)  14 us
    unnamed x34, local copies, waits for them, and re-layouts  13.1 us
    dot_general x1, matrix products, per_device(): jnp.einsum('secf,edf->secd', grad_pre, w_in, preferred_element_type=jnp.f...  8.95 us
    dot_general x1, matrix products, per_device(): jnp.einsum('secd,secf->edf', rows_all, pre_part, preferred_element_type=j...  6.13 us
  transfers between devices with their start and end apart: 2, of which 1 were waited for; matrix products, arithmetic and copies ran while one was open for 9% of the time, Pallas kernels for 27%

profile of v2, /device:TPU:0, one launch (start us, length us, event | category | flops | bytes accessed | tf_op | source)
XLA Modules:
  0.0 224.5 jit_solution(3235583261051934120)
XLA Ops:
  7.2 0.0 copy-start
  7.2 0.0 all-gather.2.cloned.1.call-start
  7.2 0.8 copy.52
  8.0 0.7 copy.53
  8.7 0.7 copy.54
  9.5 0.8 copy.61.routes
  10.3 0.8 copy.55.segment_col
  11.0 0.9 concatenate.9
  11.9 0.8 pad_maximum_fusion.refs_1_
  12.7 47.9 %shard_map.238 = (bf16[32,24,1664]{2,1,0:T(8,128)(2,1)S(1)}, bf16[32,24,1536]{2,1,0:T(8,128)(2,1)S(1)}) custom-call(bf16[24,1664]{1,0:T(8,128)(2,1)S(1)} %pad.12.refs_0_, bf16[24,1536]{1,0:T(8,128)(2,1)S(1)} %pad_maximum_fusion.refs_1_), custom_call_target="tpu_custom_call" | custom-call | tf_op jit(solution)/shard_map/pallas_call | solution.py:129
  60.6 0.0 copy-start.1
  60.6 1.5 copy-done.1
  62.1 0.0 copy-start.2
  62.1 1.4 copy-done.2
  63.5 0.0 copy-done
  63.5 0.9 convolution_bitcast_fusion.2
  64.4 0.1 pad.13.table
  64.4 0.0 copy-start.5
  64.4 0.9 copy-done.5
  65.4 0.0 copy-start.7
  65.4 0.9 copy-done.7
  66.3 0.0 copy-start.11
  66.3 0.7 copy-done.11
  66.9 8.2 %shard_map.239 = (bf16[128,768]{1,0:T(8,128)(2,1)S(1)}, bf16[128,768]{1,0:T(8,128)(2,1)S(1)}, bf16[128,768]{1,0:T(8,128)(2,1)S(1)}, bf16[128,768]{1,0:T(8,128)(2...) custom-call(bf16[128,768]{1,0:T(8,128)(2,1)S(1)} %copy-done.5, ...), custom_call_target="tpu_custom_call" | custom-call | flops 754974720 | bytes 12000000 | tf_op jit(solution)/shard_map/pallas_call | solution.py:484
  75.1 0.0 copy-start.9
  75.1 0.6 copy-done.9
  75.8 18.2 %all_to_all.10 = bf16[8,1,40,768]{3,2,1,0:T(8,128)(2,1)S(1)} all-to-all(bf16[8,1,40,768]{3,2,1,0:T(8,128)(2,1)S(1)} %bitcast.176), channel_id=1, replica_groups=mesh['dp'=4,'expert'=8] {'expert'}, dimensions={0} | all-to-all | bytes 983040 | tf_op jit(solution)/shard_map/all_to_all | solution.py:575
  93.9 0.0 copy-start.12
  93.9 5.0 %fusion.8 = f32[8,1,20,3072]{3,2,0,1:T(8,128)} fusion(bf16[1,768,3072]{2,1,0:T(8,128)(2,1)} %param.27, bf16[8,1,40,768]{3,2,0,1:T(8,128)(2,1)S(1)} %bitcast.178), kind=kOutput, calls=%fused_computation.8 | convolution fusion | flops 754974720 | bytes 6979584 | tf_op jit(solution)/shard_map/secd,edf->secf/dot_general | solution.py:579
  99.0 0.0 copy-done.12
  99.0 0.0 all-gather.2.cloned.1.call-update
  99.0 0.0 copy-start.13
  99.0 5.5 %fusion.56 = bf16[8,1,20,768]{3,2,0,1:T(8,128)(2,1)} fusion(bf16[1,3072,768]{2,1,0:T(8,128)(2,1)} %param.28, f32[8,1,20,3072]{3,2,0,1:T(8,128)} %fusion.8), kind=kOutput, calls=%fused_computation.51 | convolution fusion | flops 759521280 | bytes 6930432 | tf_op jit(solution)/shard_map/secf,efd->secd/dot_general | solution.py:581
  104.5 0.0 copy-done.13
  104.5 0.0 copy-start.6
  104.5 0.0 copy-start.8
  104.5 9.0 %fusion.61 = bf16[8,1,20,768]{3,2,0,1:T(8,128)(2,1)} fusion(bf16[1,768,3072]{2,1,0:T(8,128)(2,1)} %param.27, f32[8,1,20,3072]{3,2,0,1:T(8,128)} %fusion.8, bf16[1,3072,768]{2,1,0:T(8,128)(2,1)} %param.28, bf16[8,1,40,768]{3,2,0,1:T(8,128)(2,1)S(1)} %bitcast.179), kind=kOutput, calls=%fused_computation.52 | convolution fusion | flops 1519902720 | bytes 11943936 | tf_op jit(solution)/shard_map/secf,edf->secd/dot_general | solution.py:591
  113.4 1.9 maximum_bitcast_fusion
  115.4 4.0 %all-to-all-start.1 = ((bf16[8,1,40,768]{3,2,1,0:T(8,128)(2,1)}), bf16[8,1,40,768]{3,2,1,0:T(8,128)(2,1)S(1)}, u32[]{:S(2)}, u32[]{:S(2)}) async-start(bf16[8,1,40,768]{3,2,1,0:T(8,128)(2,1)} %maximum_bitcast_fusion), calls=%async_computation.1 | async-start | bytes 983040 | tf_op jit(solution)/shard_map/all_to_all | solution.py:595
  119.4 14.0 %all-to-all-done.1 = bf16[8,1,40,768]{3,2,1,0:T(8,128)(2,1)S(1)} async-done(((bf16[8,1,40,768]{3,2,1,0:T(8,128)(2,1)}), bf16[8,1,40,768]{3,2,1,0:T(8,128)(2,1)S(1)}, u32[]{:S(2)}, u32[]{:S(2)}) %all-to-all-start.1) | async-done | bytes 491552 | tf_op jit(solution)/shard_map/all_to_all | solution.py:595
  133.4 0.0 copy-done.6
  133.4 0.0 copy-done.8
  133.4 0.0 copy-start.10
  133.4 0.8 copy-done.10
  134.3 0.0 copy-start.14
  134.3 13.2 %shard_map.240 = (bf16[128,768]{1,0:T(8,128)(2,1)}, bf16[128,768]{1,0:T(8,128)(2,1)}, bf16[768,1664]{1,0:T(8,128)(2,1)}, bf16[768,1536]{1,0:T(8,128)(2,1)}, f32[12,256]{1,0:T(8,128)S(1)}) custom-call(bf16[128,768]{1,0:T(8,128)(2,1)S(1)} %copy-done.6, s32[128,1]{1,0:T(8,128)S(1)} %copy.61.routes, bf16[768,1664]{1,0:T(8,128)(2,1)} %bitcast.170, ...), custom_call_target="tpu_custom_call" | custom-call | flops 1509949440 | bytes 12000000 | tf_op jit(solution)/shard_map/pallas_call | solution.py:484
  147.5 0.0 copy-done.14
  147.5 0.3 fusion.78
  147.8 0.1 reshape.121
  147.9 0.0 copy-start.3
  148.0 1.7 copy-done.3
  149.7 0.0 copy-start.4
  149.7 1.7 copy-done.4
  151.3 47.3 %shard_map.241 = (f32[24,1664]{1,0:T(8,128)S(1)}, f32[24,1536]{1,0:T(8,128)S(1)}, f32[8,128]{1,0:T(8,128)S(1)}) custom-call(bf16[32,24,1664]{2,1,0:T(8,128)(2,1)S(1)} %bitcast.173, bf16[32,24,1536]{2,1,0:T(8,128)(2,1)S(1)} %bitcast.174, f32[8,128]{1,0:T(8,128)S(1)} %pad_bitcast_fusion.refs_2_), custom_call_target="tpu_custom_call" | custom-call | tf_op jit(solution)/shard_map/pallas_call | solution.py:232
  198.7 0.1 reshape.123
  198.8 0.7 copy.67
  199.4 0.7 copy.68
  200.1 0.7 slice_reduce_fusion
  200.8 0.7 fusion.107
  201.5 0.0 all-gather.2.cloned.1.call-done
  201.5 2.1 fusion.106
  203.6 3.5 %fusion.45 = f32[768,32,20]{0,1,2:T(8,128)} fusion(bf16[1,768,3072]{2,1,0:T(8,128)(2,1)} %param.27, s32[]{:T(128)S(6)} %select_n.4, bf16[32,1,20,768]{3,2,1,0:T(8,128)(2,1)S(1)} %get-tuple-element.93), kind=kOutput, calls=%fused_computation.42 | convolution fusion | flops 754974720 | bytes 4128772 | tf_op jit(solution)/shard_map/secd,edf->secf/dot_general | solution.py:623
  207.1 6.1 %convolution_bitcast_fusion.1 = f32[1,768,768]{2,1,0:T(8,128)} fusion(f32[768,32,20]{0,1,2:T(8,128)} %fusion.45, bf16[1,3072,768]{2,1,0:T(8,128)(2,1)} %param.28, s32[]{:T(128)S(6)} %select_n.4, bf16[32,1,20,768]{3,2,1,0:T(8,128)(2,1)S(1)} %get-tuple-element.93, bf16[32,1,20,768]{3,2,1,0:T(8,128)(2,1)S(1)} %get-tuple-element.92), kind=kOutput, calls=%fused_computation.38 | convolution fusion | flops 1519779840 | bytes 7471108 | tf_op jit(solution)/shard_map/secd,secf->edf/dot_general | solution.py:630
  213.2 4.4 %convolution_bitcast_fusion = f32[1,768,768]{2,1,0:T(8,128)} fusion(f32[768,32,20]{0,1,2:T(8,128)} %fusion.45, bf16[32,1,20,768]{3,2,1,0:T(8,128)(2,1)S(1)} %get-tuple-element.92), kind=kOutput, calls=%fused_computation.37 | convolution fusion | flops 759398400 | bytes 5308416 | tf_op jit(solution)/shard_map/secf,secd->efd/dot_general | solution.py:633
  (4 shorter events, 0.0 us)
Async XLA Ops:
  7.2 56.3 %copy-start = (f32[32,12]{0,1:T(8,128)S(1)}, f32[32,12]{0,1:T(8,128)}, u32[]{:S(2)}) copy-start(f32[32,12]{0,1:T(8,128)} %param.24) | copy-start | bytes 4612
  7.2 194.3 %all-gather.2.cloned.1.call-start = ((), (), s32[]{:S(2)}) async-start(), calls=%async_computation.2 | async-start | bytes 2457600 | tf_op jit(solution)/shard_map/all_gather | solution.py:576
  60.6 1.5 copy-start.1
  62.1 1.4 copy-start.2
  64.4 0.9 copy-start.5
  65.4 0.9 copy-start.7
  66.3 0.7 copy-start.11
  75.1 0.6 copy-start.9
  93.9 5.0 %copy-start.12 = (bf16[8,1,40,768]{3,2,1,0:T(8,128)(2,1)}, bf16[8,1,40,768]{3,2,1,0:T(8,128)(2,1)S(1)}, u32[]{:S(2)}) copy-start(bf16[8,1,40,768]{3,2,1,0:T(8,128)(2,1)S(1)} %all_to_all.10) | copy-start | bytes 1474564
  99.0 5.5 %copy-start.13 = (bf16[8,1,40,768]{3,2,1,0:T(8,128)(2,1)S(1)}, bf16[8,1,40,768]{3,2,1,0:T(8,128)(2,1)}, u32[]{:S(2)}) copy-start(bf16[8,1,40,768]{3,2,1,0:T(8,128)(2,1)} %copy-done.12) | copy-start | bytes 1474564
  104.5 29.0 %copy-start.6 = (bf16[128,768]{1,0:T(8,128)(2,1)S(1)}, bf16[128,768]{1,0:T(8,128)(2,1)}, u32[]{:S(2)}) copy-start(bf16[128,768]{1,0:T(8,128)(2,1)} %tokens.3) | copy-start | bytes 589828
  104.5 29.0 %copy-start.8 = (bf16[128,768]{1,0:T(8,128)(2,1)S(1)}, bf16[128,768]{1,0:T(8,128)(2,1)}, u32[]{:S(2)}) copy-start(bf16[128,768]{1,0:T(8,128)(2,1)} %cotangent.3) | copy-start | bytes 589828
  115.4 18.1 %all-to-all-start.1 = ((bf16[8,1,40,768]{3,2,1,0:T(8,128)(2,1)}), bf16[8,1,40,768]{3,2,1,0:T(8,128)(2,1)S(1)}, u32[]{:S(2)}, u32[]{:S(2)}) async-start(bf16[8,1,40,768]{3,2,1,0:T(8,128)(2,1)} %maximum_bitcast_fusion), calls=%async_computation.1 | async-start | bytes 983040 | tf_op jit(solution)/shard_map/all_to_all | solution.py:595
  133.4 0.8 copy-start.10
  134.3 13.3 %copy-start.14 = (s32[255]{0:T(256)S(1)}, s32[255]{0:T(256)}, u32[]{:S(2)}) copy-start(s32[255]{0:T(256)} %param.18) | copy-start | bytes 3064
  147.9 1.7 copy-start.3
  149.7 1.7 copy-start.4
Sparse Core Ops, SparseCore 0:
  99.1 19.9 all-gather.1

commit v3 on v2

--- a/solution.py
+++ b/solution.py
@@ -33,7 +33,22 @@
     along_z = [y_size * step for step in doubling(z_size)]
     cores = [expert_size]
     along_x = [2 * expert_size * step for step in doubling(x_size)]
-    return (along_z + along_y + along_x + cores, along_z + along_x + along_y + cores)
+    return (
+        along_z + along_y + along_x + cores,
+        along_z + along_x + along_y + cores,
+        along_y + along_x + along_z + cores,
+        along_x + along_y + along_z + cores,
+    )
+
+
+def column_parts(widths):
+    cuts = [max(128, width * 4 // 5 // 128 * 128) for width in widths]
+    return (
+        (0, 0, cuts[0]),
+        (1, 0, cuts[1]),
+        (0, cuts[0], widths[0]),
+        (1, cuts[1], widths[1]),
+    )
 
 
 def signed(me, weight):
@@ -76,18 +91,19 @@
     return copy
 
 
-def gather_kernel(orders, expert_size, *refs):
-    shards, outs, held, sems = refs[:2], refs[2:4], refs[4:6], refs[6:]
-    send_sem, recv_sem = sems
+def gather_kernel(orders, parts, expert_size, *refs):
+    shards, outs, held = refs[:2], refs[2:4], refs[4:-2]
+    send_sem, recv_sem = refs[-2:]
     me = lax.axis_index("dp") * expert_size + lax.axis_index("expert")
     stages = len(orders[0])
-    for shard, buffer in zip(shards, held):
-        buffer[0] = shard[...]
+    count = len(parts)
+    for (array, first, last), buffer in zip(parts, held):
+        buffer[0] = shards[array][:, first:last]
     meet(me, orders[0], expert_size)
-    copies = [[], []]
+    copies = [[] for _ in parts]
     for stage in range(stages):
         size = 2**stage
-        for part in range(2):
+        for part in range(count):
             if stage:
                 copies[part][-1].wait_recv()
             copies[part].append(
@@ -102,20 +118,22 @@
                 )
             )
 
-    def place(part, first, last):
+    def place(part, begin, end):
+        array, first, last = parts[part]
+
         def body(slot, carry):
-            outs[part][member(me, orders[part], slot)] = held[part][slot]
+            outs[array][member(me, orders[part], slot), :, first:last] = held[part][slot]
             return carry
 
-        lax.fori_loop(first, last, body, 0)
+        lax.fori_loop(begin, end, body, 0)
 
     half = 2 ** (stages - 1)
-    for part in range(2):
+    for part in range(count):
         place(part, 0, half)
-    for part in range(2):
+    for part in range(count):
         copies[part][-1].wait_recv()
         place(part, half, 2 * half)
-    for part in range(2):
+    for part in range(count):
         for copy in copies[part]:
             copy.wait_send()
 
@@ -125,35 +143,42 @@
     orders = exchange_orders(dp_size, expert_size)
     stages = len(orders[0])
     shapes = [(count,) + shard.shape for shard in shards]
+    parts = column_parts([shard.shape[1] for shard in shards])
     vmem = pl.BlockSpec(memory_space=pltpu.VMEM)
     return pl.pallas_call(
-        functools.partial(gather_kernel, orders, expert_size),
+        functools.partial(gather_kernel, orders, parts, expert_size),
         out_shape=[jax.ShapeDtypeStruct(shape, jnp.bfloat16) for shape in shapes],
         in_specs=[vmem] * 2,
         out_specs=[vmem] * 2,
-        scratch_shapes=[pltpu.VMEM(shape, jnp.bfloat16) for shape in shapes]
-        + [pltpu.SemaphoreType.DMA((2, stages)), pltpu.SemaphoreType.DMA((2, stages))],
+        scratch_shapes=[
+            pltpu.VMEM((count, shards[array].shape[0], last - first), jnp.bfloat16)
+            for array, first, last in parts
+        ]
+        + [pltpu.SemaphoreType.DMA((len(parts), stages))] * 2,
         compiler_params=pltpu.CompilerParams(
             collective_id=0, has_side_effects=True, vmem_limit_bytes=40 * 2**20
         ),
     )(*shards)
 
 
-def scatter_kernel(orders, expert_size, *refs):
+def scatter_kernel(orders, parts, expert_size, *refs):
+    total_parts = len(parts)
     grads, small, outs, small_out = refs[:2], refs[2], refs[3:5], refs[5]
-    held, landed, small_held, small_landed = refs[6:8], refs[8:10], refs[10], refs[11]
-    send_sem, recv_sem = refs[12:]
+    held, landed = refs[6 : 6 + total_parts], refs[6 + total_parts : 6 + 2 * total_parts]
+    small_held, small_landed, send_sem, recv_sem = refs[6 + 2 * total_parts :]
     me = lax.axis_index("dp") * expert_size + lax.axis_index("expert")
     stages = len(orders[0])
     count = 2**stages
     half = count // 2
 
-    def fill(part, first, last):
+    def fill(part, begin, end):
+        array, first, last = parts[part]
+
         def body(slot, carry):
-            held[part][slot] = grads[part][member(me, orders[part], slot)]
+            held[part][slot] = grads[array][member(me, orders[part], slot), :, first:last]
             return carry
 
-        lax.fori_loop(first, last, body, 0)
+        lax.fori_loop(begin, end, body, 0)
 
     def start(part, stage):
         size = 2**stage
@@ -174,24 +199,24 @@
             expert_size,
             small_held.at[stage],
             small_landed.at[stage],
-            send_sem.at[2, stage],
-            recv_sem.at[2, stage],
+            send_sem.at[total_parts, stage],
+            recv_sem.at[total_parts, stage],
         )
 
     small_held[stages - 1] = small[...]
     fill(0, half, count)
     meet(me, orders[0], expert_size)
-    started = [start(0, stages - 1)]
-    fill(1, half, count)
-    started.append(start(1, stages - 1))
+    current = [start(0, stages - 1)]
+    for part in range(1, total_parts):
+        fill(part, half, count)
+        current.append(start(part, stages - 1))
     small_copy = start_small(stages - 1)
-    fill(0, 0, half)
-    fill(1, 0, half)
+    for part in range(total_parts):
+        fill(part, 0, half)
     sent = []
-    current = list(started)
     for stage in reversed(range(stages)):
         size = 2**stage
-        for part in range(2):
+        for part in range(total_parts):
             current[part].wait_recv()
             sent.append(current[part])
             if stage:
@@ -207,9 +232,10 @@
                 current[part] = start(part, stage - 1)
                 lax.fori_loop(0, size // 2, body, 0)
             else:
-                outs[part][...] = held[part][0].astype(jnp.float32) + landed[part][1].astype(
-                    jnp.float32
-                )
+                array, first, last = parts[part]
+                outs[array][:, first:last] = held[part][0].astype(jnp.float32) + landed[part][
+                    1
+                ].astype(jnp.float32)
         small_copy.wait_recv()
         sent.append(small_copy)
         total = small_held[stage] + small_landed[stage]
@@ -226,11 +252,15 @@
     orders = exchange_orders(dp_size, expert_size)
     stages = len(orders[0])
     shapes = [grad.shape for grad in grads]
+    parts = column_parts([shape[2] for shape in shapes])
     vmem = pl.BlockSpec(memory_space=pltpu.VMEM)
-    buffers = [pltpu.VMEM(shape, jnp.bfloat16) for shape in shapes]
+    buffers = [
+        pltpu.VMEM(shapes[array][:2] + (last - first,), jnp.bfloat16)
+        for array, first, last in parts
+    ]
     small_buffer = pltpu.VMEM((stages,) + small.shape, jnp.float32)
     return pl.pallas_call(
-        functools.partial(scatter_kernel, orders, expert_size),
+        functools.partial(scatter_kernel, orders, parts, expert_size),
         out_shape=[jax.ShapeDtypeStruct(shape[1:], jnp.float32) for shape in shapes]
         + [jax.ShapeDtypeStruct(small.shape, jnp.float32)],
         in_specs=[vmem] * 3,
@@ -238,7 +268,7 @@
         scratch_shapes=buffers
         + buffers
         + [small_buffer] * 2
-        + [pltpu.SemaphoreType.DMA((3, stages)), pltpu.SemaphoreType.DMA((3, stages))],
+        + [pltpu.SemaphoreType.DMA((len(parts) + 1, stages))] * 2,
         compiler_params=pltpu.CompilerParams(
             collective_id=1, has_side_effects=True, vmem_limit_bytes=40 * 2**20
         ),
@@ -594,6 +624,26 @@
     results = jnp.concatenate([produced, grad_rows], axis=2)
     returned = lax.all_to_all(results, "expert", split_axis=0, concat_axis=0, tiled=True)
 
+    hidden_part = w_in.shape[2] // dp_size
+    first_hidden = lax.axis_index("dp") * hidden_part
+    in_part = lax.dynamic_slice_in_dim(w_in, first_hidden, hidden_part, axis=2)
+    out_part = lax.dynamic_slice_in_dim(w_out, first_hidden, hidden_part, axis=1)
+    pre_all = jnp.einsum("secd,edf->secf", rows_all, in_part, preferred_element_type=jnp.float32)
+    act_all, pull_all = jax.vjp(gelu_tanh, pre_all)
+    grad_hidden_all = jnp.einsum(
+        "secd,efd->secf", grads_all, out_part, preferred_element_type=jnp.float32
+    )
+    pre_part = pull_all(grad_hidden_all)[0].astype(jnp.bfloat16)
+    act_part = act_all.astype(jnp.bfloat16)
+    grad_first_w = jnp.einsum(
+        "secd,secf->edf", rows_all, pre_part, preferred_element_type=jnp.float32
+    )
+    grad_second_w = jnp.einsum(
+        "secf,secd->efd", act_part, grads_all, preferred_element_type=jnp.float32
+    )
+    returned, grad_first_w, grad_second_w = lax.optimization_barrier(
+        (returned, grad_first_w, grad_second_w)
+    )
     output, grad_inputs, send_one, send_two, grad_offsets = local_call(
         functools.partial(backward_kernel, experts, num_heads),
         (
@@ -616,23 +666,6 @@
         flops=10 * dense_flops,
     )
     grad_rel = jnp.dot(onehot.T, grad_offsets[:, :-1].T, precision=highest)
-    hidden_part = w_in.shape[2] // dp_size
-    first_hidden = lax.axis_index("dp") * hidden_part
-    in_part = lax.dynamic_slice_in_dim(w_in, first_hidden, hidden_part, axis=2)
-    out_part = lax.dynamic_slice_in_dim(w_out, first_hidden, hidden_part, axis=1)
-    pre_all = jnp.einsum("secd,edf->secf", rows_all, in_part, preferred_element_type=jnp.float32)
-    act_all, pull_all = jax.vjp(gelu_tanh, pre_all)
-    grad_hidden_all = jnp.einsum(
-        "secd,efd->secf", grads_all, out_part, preferred_element_type=jnp.float32
-    )
-    pre_part = pull_all(grad_hidden_all)[0].astype(jnp.bfloat16)
-    act_part = act_all.astype(jnp.bfloat16)
-    grad_first_w = jnp.einsum(
-        "secd,secf->edf", rows_all, pre_part, preferred_element_type=jnp.float32
-    )
-    grad_second_w = jnp.einsum(
-        "secf,secd->efd", act_part, grads_all, preferred_element_type=jnp.float32
-    )
     entries = grad_rel.size
     small_rows = -(-entries // 1024) * 8
     small = jnp.pad(grad_rel.reshape(-1), (0, small_rows * 128 - entries))

time: 225 us -> 194 us (0.86)
  Pallas kernels: 117 us -> 101 us
  waiting for transfers between devices: 14.1 us -> 0.03 us
  matrix products: 34.6 us -> 30.7 us
  local copies, waits for them, and re-layouts: 20 us -> 22.6 us
    pallas_call x2, Pallas kernels: 95.2 us -> 79.8 us  [the longest x1 40.8 us: gather_shards(): pl.pallas_call(functools.partial(gather_kernel, orders, parts, expert_siz...]
    all_to_all x1, waiting for transfers between devices: 14 us -> 0.01 us  [per_device(): lax.all_to_all(results, 'expert', split_axis=0, concat_axis=0, tiled=True)]
    dot_general x1, matrix products: 5.49 us -> 1.68 us  [per_device(): jnp.einsum('secf,efd->secd', hidden_act.astype(jnp.bfloat16), w_out, pref...]
    unnamed x34 -> x38, local copies, waits for them, and re-layouts: 13.1 us -> 14.5 us
  transfers between devices with their start and end apart: 2 -> 2, of which waited for: 1 -> 0; matrix products, arithmetic and copies ran while one was open for 9% -> 18% of each run, Pallas kernels for 27% -> 0%
where the time goes in v3:
time: 194 us; the launch traced here: 193 us
  Pallas kernels  101 us (52%)
  matrix products  30.7 us (16%)
  local copies, waits for them, and re-layouts  22.6 us (12%)
  blocking collectives  18 us (9%)
  between operations  14.2 us (7%)
  starting transfers between devices  4.1 us (2%)
  other arithmetic  2.63 us (1%)
    pallas_call x1, Pallas kernels, gather_shards(): pl.pallas_call(functools.partial(gather_kernel, orders, parts, expert_siz...  40.8 us
    pallas_call x1, Pallas kernels, scatter_sums(): pl.pallas_call(functools.partial(scatter_kernel, orders, parts, expert_si...  39 us
    pallas_call x2, Pallas kernels, local_call(): pl.pallas_call(kernel, out_shape=[jax.ShapeDtypeStruct(shape, dtype) for...  21.4 us
    all_to_all x1, blocking collectives, per_device(): lax.all_to_all(outgoing, 'expert', split_axis=0, concat_axis=0, tiled=True)  18 us
    unnamed x38, local copies, waits for them, and re-layouts  14.5 us
    dot_general x1, matrix products, per_device(): jnp.einsum('secf,edf->secd', grad_pre, w_in, preferred_element_type=jnp.f...  8.64 us
    dot_general x1, matrix products, per_device(): jnp.einsum('secd,secf->edf', rows_all, pre_part, preferred_element_type=j...  6.85 us
    dot_general x1, matrix products, per_device(): jnp.einsum('secf,secd->efd', act_part, grads_all, preferred_element_type=...  4.77 us
  transfers between devices with their start and end apart: 2, of which 0 were waited for; matrix products, arithmetic and copies ran while one was open for 18% of the time, Pallas kernels for 0%

profile of v3, /device:TPU:0, one launch (start us, length us, event | category | flops | bytes accessed | tf_op | source)
XLA Modules:
  0.0 193.4 jit_solution(733990153123248988)
XLA Ops:
  7.2 0.0 copy-start
  7.2 0.0 all-gather.2.cloned.1.call-start
  7.2 0.7 copy.53
  8.0 0.7 copy.54
  8.7 0.8 copy.52
  9.5 0.8 copy.65.routes
  10.3 0.8 copy.55.segment_col
  11.0 0.0 copy-done
  11.0 0.9 convolution_bitcast_fusion.2
  11.9 0.1 pad.13.table
  12.0 0.9 concatenate.9
  12.9 0.8 pad_maximum_fusion.refs_1_
  13.7 40.8 %shard_map.238 = (bf16[32,24,1664]{2,1,0:T(8,128)(2,1)S(1)}, bf16[32,24,1536]{2,1,0:T(8,128)(2,1)S(1)}) custom-call(bf16[24,1664]{1,0:T(8,128)(2,1)S(1)} %pad.12.refs_0_, bf16[24,1536]{1,0:T(8,128)(2,1)S(1)} %pad_maximum_fusion.refs_1_), custom_call_target="tpu_custom_call" | custom-call | tf_op jit(solution)/shard_map/pallas_call | solution.py:148
  54.5 0.0 copy-start.1
  54.5 1.5 copy-done.1
  56.0 0.0 copy-start.2
  56.0 1.4 copy-done.2
  57.4 0.0 copy-start.5
  57.4 0.9 copy-done.5
  58.3 0.0 copy-start.7
  58.3 0.9 copy-done.7
  59.3 0.0 copy-start.11
  59.3 0.7 copy-done.11
  59.9 8.2 %shard_map.239 = (bf16[128,768]{1,0:T(8,128)(2,1)S(1)}, bf16[128,768]{1,0:T(8,128)(2,1)S(1)}, bf16[128,768]{1,0:T(8,128)(2,1)S(1)}, bf16[128,768]{1,0:T(8,128)(2...) custom-call(bf16[128,768]{1,0:T(8,128)(2,1)S(1)} %copy-done.5, ...), custom_call_target="tpu_custom_call" | custom-call | flops 754974720 | bytes 12000000 | tf_op jit(solution)/shard_map/pallas_call | solution.py:514
  68.1 0.0 copy-start.9
  68.1 0.6 copy-done.9
  68.7 18.0 %all_to_all.10 = bf16[8,1,40,768]{3,2,1,0:T(8,128)(2,1)} all-to-all(bf16[8,1,40,768]{3,2,1,0:T(8,128)(2,1)S(1)} %bitcast.176), channel_id=1, replica_groups=mesh['dp'=4,'expert'=8] {'expert'}, dimensions={0} | all-to-all | bytes 983040 | tf_op jit(solution)/shard_map/all_to_all | solution.py:605
  86.7 0.0 all-gather.2.cloned.1.call-update
  86.7 0.0 copy-start.15
  86.7 3.7 %fusion.8 = f32[8,1,20,3072]{3,2,0,1:T(8,128)S(1)} fusion(bf16[1,768,3072]{2,1,0:T(8,128)(2,1)} %param.27, bf16[8,1,40,768]{3,2,0,1:T(8,128)(2,1)} %bitcast.178), kind=kOutput, calls=%fused_computation.8 | convolution fusion | flops 754974720 | bytes 6979584 | tf_op jit(solution)/shard_map/secd,edf->secf/dot_general | solution.py:609
  90.4 0.0 copy-start.13
  90.4 1.4 copy-done.13
  91.8 0.0 copy-done.15
  91.8 0.0 copy-start.12
  91.8 1.7 fusion.56
  93.5 0.0 copy-done.12
  93.5 8.6 %fusion.61 = bf16[8,1,20,768]{3,2,0,1:T(8,128)(2,1)} fusion(bf16[1,768,3072]{2,1,0:T(8,128)(2,1)} %param.27, f32[8,1,20,3072]{3,2,0,1:T(8,128)} %copy-done.13, bf16[1,3072,768]{2,1,0:T(8,128)(2,1)} %param.28, bf16[8,1,40,768]{3,2,0,1:T(8,128)(2,1)S(1)} %bitcast.179), kind=kOutput, calls=%fused_computation.52 | convolution fusion | flops 1519902720 | bytes 11943936 | tf_op jit(solution)/shard_map/secf,edf->secd/dot_general | solution.py:621
  102.1 1.8 maximum_bitcast_fusion
  104.0 4.1 %all-to-all-start.1 = ((bf16[8,1,40,768]{3,2,1,0:T(8,128)(2,1)}), bf16[8,1,40,768]{3,2,1,0:T(8,128)(2,1)S(1)}, u32[]{:S(2)}, u32[]{:S(2)}) async-start(bf16[8,1,40,768]{3,2,1,0:T(8,128)(2,1)} %maximum_bitcast_fusion), calls=%async_computation.1 | async-start | bytes 983040 | tf_op jit(solution)/shard_map/all_to_all | solution.py:625
  108.0 0.0 all-gather.2.cloned.1.call-done
  108.1 3.2 %fusion.106 = (bf16[32,1,20,768]{3,2,1,0:T(8,128)(2,1)}, bf16[32,1,20,768]{3,2,1,0:T(8,128)(2,1)S(1)}) fusion(bf16[32,1,40,768]{3,2,1,0:T(8,128)(2,1)} %all-gather.2.cloned.1.call-done), kind=kLoop, calls=%fused_computation.101 | loop fusion | bytes 3932160 | tf_op jit(solution)/shard_map/slice | solution.py:608
  111.3 0.0 copy-start.14
  111.3 3.9 %fusion.45 = f32[768,32,20]{0,1,2:T(8,128)} fusion(bf16[1,768,3072]{2,1,0:T(8,128)(2,1)} %param.27, s32[]{:T(128)S(6)} %select_n.4, bf16[32,1,20,768]{3,2,1,0:T(8,128)(2,1)S(1)} %get-tuple-element.99), kind=kOutput, calls=%fused_computation.42 | convolution fusion | flops 754974720 | bytes 4128772 | tf_op jit(solution)/shard_map/secd,edf->secf/dot_general | solution.py:631
  115.2 0.0 copy-done.14
  115.2 6.9 %convolution_bitcast_fusion.1 = f32[1,768,768]{2,1,0:T(8,128)} fusion(f32[768,32,20]{0,1,2:T(8,128)} %fusion.45, bf16[1,3072,768]{2,1,0:T(8,128)(2,1)} %param.28, s32[]{:T(128)S(6)} %select_n.4, bf16[32,1,20,768]{3,2,1,0:T(8,128)(2,1)} %copy-done.14, bf16[32,1,20,768]{3,2,1,0:T(8,128)(2,1)} %get-tuple-element.98), kind=kOutput, calls=%fused_computation.38 | convolution fusion | flops 1519779840 | bytes 7864324 | tf_op jit(solution)/shard_map/secd,secf->edf/dot_general | solution.py:638
  122.1 4.8 %convolution_bitcast_fusion = f32[1,768,768]{2,1,0:T(8,128)} fusion(f32[768,32,20]{0,1,2:T(8,128)} %fusion.45, bf16[32,1,20,768]{3,2,1,0:T(8,128)(2,1)} %get-tuple-element.98), kind=kOutput, calls=%fused_computation.37 | convolution fusion | flops 759398400 | bytes 5308416 | tf_op jit(solution)/shard_map/secf,secd->efd/dot_general | solution.py:641
  126.8 0.0 all-to-all-done.1
  126.8 0.0 copy-done.6
  126.8 0.0 copy-done.8
  126.8 0.0 copy-start.10
  126.9 0.8 copy-done.10
  127.7 13.3 %shard_map.240 = (bf16[128,768]{1,0:T(8,128)(2,1)}, bf16[128,768]{1,0:T(8,128)(2,1)}, bf16[768,1664]{1,0:T(8,128)(2,1)}, bf16[768,1536]{1,0:T(8,128)(2,1)}, f32[12,256]{1,0:T(8,128)S(1)}) custom-call(bf16[128,768]{1,0:T(8,128)(2,1)S(1)} %copy-done.6, s32[128,1]{1,0:T(8,128)S(1)} %copy.65.routes, bf16[768,1664]{1,0:T(8,128)(2,1)} %bitcast.170, ...), custom_call_target="tpu_custom_call" | custom-call | flops 1509949440 | bytes 12000000 | tf_op jit(solution)/shard_map/pallas_call | solution.py:514
  140.9 0.0 copy-done.16
  140.9 0.3 fusion.78
  141.2 0.1 reshape.127
  141.4 0.0 copy-start.3
  141.4 1.7 copy-done.3
  143.1 1.7 copy-done.4
  144.8 39.0 %shard_map.241 = (f32[24,1664]{1,0:T(8,128)S(1)}, f32[24,1536]{1,0:T(8,128)S(1)}, f32[8,128]{1,0:T(8,128)S(1)}) custom-call(bf16[32,24,1664]{2,1,0:T(8,128)(2,1)S(1)} %bitcast.173, bf16[32,24,1536]{2,1,0:T(8,128)(2,1)S(1)} %bitcast.174, f32[8,128]{1,0:T(8,128)S(1)} %pad_bitcast_fusion.refs_2_), custom_call_target="tpu_custom_call" | custom-call | tf_op jit(solution)/shard_map/pallas_call | solution.py:262
  183.7 0.7 slice_reduce_fusion
  184.4 0.7 fusion.107
  185.2 0.7 copy.68
  185.8 0.1 reshape.129
  185.9 0.7 copy.67
  (8 shorter events, 0.0 us)
Async XLA Ops:
  7.2 3.8 %copy-start = (f32[32,12]{0,1:T(8,128)S(1)}, f32[32,12]{0,1:T(8,128)}, u32[]{:S(2)}) copy-start(f32[32,12]{0,1:T(8,128)} %param.24) | copy-start | bytes 4612
  7.2 100.9 %all-gather.2.cloned.1.call-start = ((), (), s32[]{:S(2)}) async-start(), calls=%async_computation.2 | async-start | bytes 2457600 | tf_op jit(solution)/shard_map/all_gather | solution.py:606
  54.5 1.5 copy-start.1
  56.0 1.4 copy-start.2
  57.4 0.9 copy-start.5
  58.3 0.9 copy-start.7
  59.3 0.7 copy-start.11
  68.1 0.6 copy-start.9
  86.7 5.1 %copy-start.15 = (bf16[1,3072,768]{2,1,0:T(8,128)(2,1)S(1)}, bf16[1,3072,768]{2,1,0:T(8,128)(2,1)}, u32[]{:S(2)}) copy-start(bf16[1,3072,768]{2,1,0:T(8,128)(2,1)} %param.28) | copy-start | bytes 14155780
  90.4 1.4 copy-start.13
  91.8 1.7 copy-start.12
  104.0 22.9 %all-to-all-start.1 = ((bf16[8,1,40,768]{3,2,1,0:T(8,128)(2,1)}), bf16[8,1,40,768]{3,2,1,0:T(8,128)(2,1)S(1)}, u32[]{:S(2)}, u32[]{:S(2)}) async-start(bf16[8,1,40,768]{3,2,1,0:T(8,128)(2,1)} %maximum_bitcast_fusion), calls=%async_computation.1 | async-start | bytes 983040 | tf_op jit(solution)/shard_map/all_to_all | solution.py:625
  111.3 3.9 %copy-start.14 = (bf16[32,1,20,768]{3,2,1,0:T(8,128)(2,1)}, bf16[32,1,20,768]{3,2,1,0:T(8,128)(2,1)S(1)}, u32[]{:S(2)}) copy-start(bf16[32,1,20,768]{3,2,1,0:T(8,128)(2,1)S(1)} %get-tuple-element.99) | copy-start | bytes 2949124
  122.1 4.8 %copy-start.6 = (bf16[128,768]{1,0:T(8,128)(2,1)S(1)}, bf16[128,768]{1,0:T(8,128)(2,1)}, u32[]{:S(2)}) copy-start(bf16[128,768]{1,0:T(8,128)(2,1)} %tokens.3) | copy-start | bytes 589828
  122.1 4.8 %copy-start.8 = (bf16[128,768]{1,0:T(8,128)(2,1)S(1)}, bf16[128,768]{1,0:T(8,128)(2,1)}, u32[]{:S(2)}) copy-start(bf16[128,768]{1,0:T(8,128)(2,1)} %cotangent.3) | copy-start | bytes 589828
  126.8 0.8 copy-start.10
  127.7 13.3 %copy-start.16 = (s32[255]{0:T(256)S(1)}, s32[255]{0:T(256)}, u32[]{:S(2)}) copy-start(s32[255]{0:T(256)} %param.18) | copy-start | bytes 3064
  141.4 1.7 copy-start.3
  143.1 1.7 copy-start.4
Sparse Core Ops, SparseCore 0:
  86.8 19.9 all-gather.1
